TPU v7x, 256 devices: a whole 4x4x8 slice. The times are simulated.
256 devices in a mesh: depth: 8 (over x, z_hi), pos: 32 (over y, z_lo, core).
Axes of the slice: x: 4, y: 4, z: 8 (z_hi: 2, z_lo: 4; z = z_hi * 4 + z_lo), core: 2. Of those that a mesh axis runs over, the one named last changes fastest.
Arguments:
- object_slices: bfloat16 [8, 256, 2, 256], P('depth', 'pos'), may hold values from -1 to 2, as said below
- probe_wave: float32 [2, 128, 128], replicated, may hold values from -6 to 6
- propagator_phase: float32 [128, 128], replicated, may hold values from -3.140625 to 3.140625
- measured: float32 [1024, 128, 128], P(('depth', 'pos')), may hold values from 0.5 to 4
- offsets: int32 [1024, 2], P(('depth', 'pos')), may hold values from 0 to 128
- slice_order: int32 [8], replicated, may hold values from 0 to 7, each once
Outputs:
- object_grad: float32 [8, 256, 2, 256], P('depth', 'pos')
Inputs may be any that keep to these rules, and one draw needn't show every extreme that they name: `object_slices`: the real parts lie around 1 and the imaginary parts around 0.
All inputs are finite; a program needn't handle non-finite values.
Results may differ from a plain program's by a relative error of at most 0.0003.
Values may be sent and summed in bfloat16 or wider, within the bound.
A program may use at most 128 MiB of HBM per device.

v0:
```python
import math

import jax
import jax.numpy as jnp
from jax import lax
from jax.sharding import PartitionSpec as P

HIGHEST = lax.Precision.HIGHEST


def fourier_tables(length):
    counter = jnp.arange(length, dtype=jnp.int32)
    product = counter[:, None] * counter[None, :] % length
    angle = -2.0 * math.pi / length * product.astype(jnp.float32)
    factor = 1.0 / math.sqrt(length)
    return (jnp.cos(angle) * factor, jnp.sin(angle) * factor)


def complex_times(left_real, left_imag, right_real, right_imag):
    return (
        left_real * right_real - left_imag * right_imag,
        left_real * right_imag + left_imag * right_real,
    )


def fourier_map(wave_real, wave_imag, table_real, table_imag):
    inner_real = jnp.einsum("jk,pkl->pjl", table_real, wave_real, precision=HIGHEST) - jnp.einsum(
        "jk,pkl->pjl", table_imag, wave_imag, precision=HIGHEST
    )
    inner_imag = jnp.einsum("jk,pkl->pjl", table_real, wave_imag, precision=HIGHEST) + jnp.einsum(
        "jk,pkl->pjl", table_imag, wave_real, precision=HIGHEST
    )
    outer_real = jnp.einsum("pjk,kl->pjl", inner_real, table_real, precision=HIGHEST) - jnp.einsum(
        "pjk,kl->pjl", inner_imag, table_imag, precision=HIGHEST
    )
    outer_imag = jnp.einsum("pjk,kl->pjl", inner_real, table_imag, precision=HIGHEST) + jnp.einsum(
        "pjk,kl->pjl", inner_imag, table_real, precision=HIGHEST
    )
    return (outer_real, outer_imag)


def per_device(object_slices, probe_wave, propagator_phase, measured, offsets, slice_order):
    width = object_slices.shape[3]
    length = probe_wave.shape[1]
    row_blocks = lax.all_gather(object_slices, "pos", axis=1, tiled=True)
    whole = lax.all_gather(row_blocks, "depth", axis=0, tiled=True)
    layers = whole.shape[0]
    positions_total = offsets.shape[0] * lax.axis_size("depth") * lax.axis_size("pos")
    factor = 0.25 * width / (length * math.sqrt(positions_total))
    anchor = jnp.zeros((), jnp.int32)

    def cut_window(corner):
        return lax.dynamic_slice(
            whole, (anchor, corner[0], anchor, corner[1]), (layers, length, 2, length)
        )

    windows = jnp.take(jax.vmap(cut_window)(offsets), slice_order, axis=1).astype(jnp.float32)
    table_real, table_imag = fourier_tables(length)
    kernel_real = jnp.cos(propagator_phase)
    kernel_imag = jnp.sin(propagator_phase)

    def layer_step(wave_real, wave_imag, trans_real, trans_imag):
        mixed_real, mixed_imag = complex_times(trans_real, trans_imag, wave_real, wave_imag)
        freq_real, freq_imag = fourier_map(mixed_real, mixed_imag, table_real, table_imag)
        freq_real, freq_imag = complex_times(freq_real, freq_imag, kernel_real, kernel_imag)
        return fourier_map(freq_real, freq_imag, table_real, -table_imag)

    def misfit(window_set):
        count = window_set.shape[0]
        wave_real = jnp.broadcast_to(probe_wave[0], (count, length, length))
        wave_imag = jnp.broadcast_to(probe_wave[1], (count, length, length))
        for layer in range(layers - 1):
            wave_real, wave_imag = layer_step(
                wave_real, wave_imag, window_set[:, layer, :, 0, :], window_set[:, layer, :, 1, :]
            )
        exit_real, exit_imag = complex_times(
            window_set[:, layers - 1, :, 0, :],
            window_set[:, layers - 1, :, 1, :],
            wave_real,
            wave_imag,
        )
        far_real, far_imag = fourier_map(exit_real, exit_imag, table_real, table_imag)
        intensity = far_real * far_real + far_imag * far_imag
        return 0.5 * factor * jnp.sum((intensity - measured) ** 2)

    unused, pullback = jax.vjp(misfit, windows)
    (window_grads,) = pullback(jnp.ones((), jnp.float32))
    inverse = jnp.argsort(slice_order)
    window_grads = jnp.take(window_grads, inverse, axis=1)

    def add_window(position, total):
        corner = offsets[position]
        start = (anchor, corner[0], anchor, corner[1])
        piece = lax.dynamic_slice(total, start, (layers, length, 2, length))
        piece = piece + lax.dynamic_index_in_dim(window_grads, position, 0, keepdims=False)
        return lax.dynamic_update_slice(total, piece, start)

    partial_grad = lax.fori_loop(
        0, offsets.shape[0], add_window, jnp.zeros((layers, width, 2, width), jnp.float32)
    )
    owners = lax.psum_scatter(partial_grad, "depth", scatter_dimension=0, tiled=True)
    return lax.psum_scatter(owners, "pos", scatter_dimension=1, tiled=True)


def solution(mesh):
    in_specs = (
        P("depth", "pos", None, None),
        P(),
        P(),
        P(("depth", "pos"), None, None),
        P(("depth", "pos"), None),
        P(),
    )
    out_specs = P("depth", "pos", None, None)
    return jax.shard_map(
        per_device, mesh=mesh, in_specs=in_specs, out_specs=out_specs, check_vma=False
    )
```

profile of v0, /device:TPU:2, one launch (start us, length us, event | category | flops | bytes accessed | tf_op | source)
XLA Modules:
  0.0 715.1 jit_solution(27022487274564380)
XLA Ops:
  6.5 45.9 %all_gather.6 = bf16[1,256,2,256]{3,2,0,1:T(2,128)(2,1)S(1)} all-gather(bf16[1,8,2,256]{3,2,0,1:T(2,128)(2,1)} %bitcast.1097), channel_id=1, replica_groups=mesh['depth'=8,'pos'=32] {'pos'}, dimensions={1}, use_global_device_ids=true | all-gather | bytes 270336 | tf_op jit(solution)/shard_map/all_gather | solution.py:45
  59.3 67.6 %all-gather.2.cloned.1.call-done = bf16[8,256,2,256]{3,1,2,0:T(8,128)(2,1)} async-done(((bf16[1,256,2,256]{3,1,2,0:T(8,128)(2,1)}), bf16[8,256,2,256]{3,1,2,0:T(8,128)(2,1)}) %all-gather.2.cloned.1.call-update) | async-done | bytes 2097168 | tf_op jit(solution)/shard_map/all_gather | solution.py:46
  126.8 20.8 %while.15 = (s32[]{:T(128)}, bf16[8,256,2,256]{3,1,2,0:T(8,128)(2,1)}, s32[4,4]{1,0:T(4,128)S(1)}, bf16[4,8,128,2,128]{4,2,3,1,0:T(8,128)(2,1)}, s32[]{:T(128)}) while((s32[]{:T(128)}, bf16[8,256,2,256]{3,1,2,0:T(8,128)(2,1)}, s32[4,4]{1,0:T(4,128)S(1)}, bf16[4,8,128,2,128]{4,2,3,1,0:T(8,128)(2,1)}, s32[]{:T(128)}) %tuple.96), condition=%wide.while_cond, body=%wide.while_body.sunk | while | flops 2 | bytes 3145861 | solution.py:53
  127.5 3.1 constant_dynamic-slice_fusion.14
  132.7 3.1 constant_dynamic-slice_fusion.14
  137.9 3.1 constant_dynamic-slice_fusion.14
  143.1 3.1 constant_dynamic-slice_fusion.14
  147.7 2.5 gather_fusion
  264.2 1.8 add_bitcast_fusion.13
  335.2 2.5 pad_add_fusion
  337.7 5.0 gather_fusion.1
  342.7 4.9 select_bitcast_fusion
  347.6 2.4 broadcast_in_dim.119.clone
  350.0 92.1 %while.14 = (s32[]{:T(128)}, f32[8,256,2,256]{3,1,2,0:T(8,128)}, s32[4,2]{0,1:T(2,128)S(1)}, f32[4,8,128,2,128]{4,2,0,3,1:T(8,128)}, s32[]{:T(128)}, /*index=5*/s32[]{:T(128)}, s32[]{:T(128)}) while((s32[]{:T(128)}, f32[8,256,2,256]{3,1,2,0:T(8,128)}, s32[4,2]{0,1:T(2,128)S(1)}, f32[4,8,128,2,128]{4,2,0,3,1:T(8,128)}, s32[]{:T(128)}, ...), condition=%wide.region_2.3_spmd, body=%wide.region_1.2_spmd.sunk | while | flops 262152 | bytes 11534541 | solution.py:98
  355.8 2.0 constant_dynamic-slice_fusion.11
  359.3 14.1 %dynamic_update_slice.8 = f32[8,256,2,256]{3,1,2,0:T(8,128)} dynamic-update-slice(f32[8,256,2,256]{3,1,2,0:T(8,128)} %get-tuple-element.285, f32[8,128,2,128]{3,1,2,0:T(8,128)S(1)} %copy.1031, s32[]{:T(128)} %constant.79.clone.1..sunk, s32[]{:T(128)S(6)} %select_n.1317, s32[]{:T(128)} %constant.79.clone.1..sunk, s32[]{:T(128)S(6)} %select_n.1318) | dynamic-update-slice | bytes 2097156 | tf_op jit(solution)/shard_map/while/body/eval_jaxpr/dynamic_update_slice | solution.py:96
  379.0 2.0 constant_dynamic-slice_fusion.11
  382.5 14.1 %dynamic_update_slice.8 = f32[8,256,2,256]{3,1,2,0:T(8,128)} dynamic-update-slice(f32[8,256,2,256]{3,1,2,0:T(8,128)} %get-tuple-element.285, f32[8,128,2,128]{3,1,2,0:T(8,128)S(1)} %copy.1031, s32[]{:T(128)} %constant.79.clone.1..sunk, s32[]{:T(128)S(6)} %select_n.1317, s32[]{:T(128)} %constant.79.clone.1..sunk, s32[]{:T(128)S(6)} %select_n.1318) | dynamic-update-slice | bytes 2097156 | tf_op jit(solution)/shard_map/while/body/eval_jaxpr/dynamic_update_slice | solution.py:96
  402.2 2.0 constant_dynamic-slice_fusion.11
  405.7 13.4 %dynamic_update_slice.8 = f32[8,256,2,256]{3,1,2,0:T(8,128)} dynamic-update-slice(f32[8,256,2,256]{3,1,2,0:T(8,128)} %get-tuple-element.285, f32[8,128,2,128]{3,1,2,0:T(8,128)S(1)} %copy.1031, s32[]{:T(128)} %constant.79.clone.1..sunk, s32[]{:T(128)S(6)} %select_n.1317, s32[]{:T(128)} %constant.79.clone.1..sunk, s32[]{:T(128)S(6)} %select_n.1318) | dynamic-update-slice | bytes 2097156 | tf_op jit(solution)/shard_map/while/body/eval_jaxpr/dynamic_update_slice | solution.py:96
  424.8 2.0 constant_dynamic-slice_fusion.11
  428.2 13.8 %dynamic_update_slice.8 = f32[8,256,2,256]{3,1,2,0:T(8,128)} dynamic-update-slice(f32[8,256,2,256]{3,1,2,0:T(8,128)} %get-tuple-element.285, f32[8,128,2,128]{3,1,2,0:T(8,128)S(1)} %copy.1031, s32[]{:T(128)} %constant.79.clone.1..sunk, s32[]{:T(128)S(6)} %select_n.1317, s32[]{:T(128)} %constant.79.clone.1..sunk, s32[]{:T(128)S(6)} %select_n.1318) | dynamic-update-slice | bytes 2097156 | tf_op jit(solution)/shard_map/while/body/eval_jaxpr/dynamic_update_slice | solution.py:96
  442.1 122.2 %reduce-scatter.5.cloned.1.call-done = f32[1,256,2,256]{3,1,2,0:T(8,128)} async-done(((f32[8,256,2,256]{3,1,2,0:T(8,128)}), f32[1,256,2,256]{3,1,2,0:T(8,128)}) %reduce-scatter.5.cloned.1.call-update) | async-done | bytes 524304 | tf_op jit(solution)/shard_map/reduce_scatter | solution.py:101
  566.7 140.3 %reduce-scatter.7.cloned.1.call-done = f32[8,512]{1,0:T(8,128)} async-done(((f32[256,512]{1,0:T(8,128)}), f32[8,512]{1,0:T(8,128)}) %reduce-scatter.7.cloned.1.call-update) | async-done | bytes 16400
  (309 shorter events, 213.8 us)
Async XLA Ops:
  6.5 120.3 %all-gather.2.cloned.1.call-start = ((), (), s32[]{:S(2)}) async-start(), calls=%async_computation.2 | async-start | bytes 2359296 | tf_op jit(solution)/shard_map/all_gather | solution.py:46
  53.2 511.2 %reduce-scatter.5.cloned.1.call-start = ((), (), s32[]{:S(2)}) async-start(), calls=%async_computation.3 | async-start | bytes 4718592 | tf_op jit(solution)/shard_map/reduce_scatter | solution.py:101
  150.6 11.8 %copy-start = (f32[4,8,128,2,128]{4,2,0,3,1:T(8,128)}, f32[4,8,128,2,128]{4,2,0,3,1:T(8,128)S(1)}, u32[]{:S(2)}) copy-start(f32[4,8,128,2,128]{4,2,0,3,1:T(8,128)S(1)} %convert_bitcast_fusion) | copy-start | bytes 12582916
  239.6 8.3 %copy-start.1 = (f32[4,128,128]{2,1,0:T(8,128)S(1)}, f32[4,128,128]{2,1,0:T(8,128)}, u32[]{:S(2)}) copy-start(f32[4,128,128]{2,1,0:T(8,128)} %param.11) | copy-start | bytes 786436
  347.6 2.4 copy-start.2
  442.1 265.0 %reduce-scatter.7.cloned.1.call-start = ((), (), s32[]{:S(2)}) async-start(), calls=%async_computation.4 | async-start | bytes 540672
Sparse Core Ops, SparseCore 0:
  53.3 73.5 all-gather.1
  442.2 122.1 reduce-scatter.4
  566.9 140.1 reduce-scatter.6
where the time goes:
time: 729 us; the launch traced here: 715 us
  waiting for transfers between devices  330 us (45%)
  matrix products  183 us (25%)
  local copies, waits for them, and re-layouts  110 us (15%)
  blocking collectives  45.9 us (6%)
  other arithmetic  16.2 us (2%)
  between operations  15.3 us (2%)
  loops' own time  15.2 us (2%)
    unnamed x4, waiting for transfers between devices  140 us
    reduce_scatter x1, waiting for transfers between devices, per_device(): lax.psum_scatter(partial_grad, 'depth', scatter_dimension=0, tiled=True)  122 us
    all_gather x1, waiting for transfers between devices, per_device(): whole = lax.all_gather(row_blocks, 'depth', axis=0, tiled=True)  67.6 us
    dynamic_update_slice x8, local copies, waits for them, and re-layouts, add_window(): return lax.dynamic_update_slice(total, piece, start)  55.8 us
    all_gather x1, blocking collectives, per_device(): row_blocks = lax.all_gather(object_slices, 'pos', axis=1, tiled=True)  45.9 us
    dot_general x30, matrix products, fourier_map(): jnp.einsum('jk,pkl->pjl', table_imag, wave_imag, precision=HIGHEST)  29.3 us
    dot_general x30, matrix products, fourier_map(): jnp.einsum('pjk,kl->pjl', inner_imag, table_imag, precision=HIGHEST)  26.4 us
    dot_general x30, matrix products, fourier_map(): jnp.einsum('jk,pkl->pjl', table_imag, wave_real, precision=HIGHEST)  21.8 us
  transfers between devices with their start and end apart: 3, of which 3 were waited for; matrix products, arithmetic and copies ran while one was open for 1% of the time, Pallas kernels for 0%

commit v1 on v0

v1 whole, which is shorter than its diff:
```python
import functools
import math

import jax
import jax.numpy as jnp
import ml_dtypes
import numpy as np
from jax import lax
from jax.experimental import pallas as pl
from jax.experimental.pallas import tpu as pltpu
from jax.sharding import PartitionSpec as P

BF16 = jnp.bfloat16
F32 = jnp.float32
X, ZH, Y, ZL = 4, 2, 4, 4
Z = ZH * ZL


class Place:
    def __init__(self):
        depth, pos = lax.axis_index("depth"), lax.axis_index("pos")
        self.depth = depth
        self.x, self.zh = depth // ZH, depth % ZH
        self.core = pos % 2
        self.yz = pos // 2
        self.y, self.zl = self.yz // ZL, self.yz % ZL
        self.z = self.zh * ZL + self.zl

    def device(self, x=None, y=None, z=None, core=None):
        x = self.x if x is None else x
        y = self.y if y is None else y
        z = self.z if z is None else z
        core = self.core if core is None else core
        return (x * ZH + z // ZL, (y * ZL + z % ZL) * 2 + core)

    def xs(self, d):
        return (self.x + d) % X

    def ys(self, d):
        return (self.y + d) % Y

    def zs(self, d):
        return (self.z + d) % Z


def greet(me):
    barrier = pltpu.get_barrier_semaphore()
    partners = [me.device(core=1 - me.core)]
    partners += [me.device(x=me.xs(d)) for d in range(1, X)]
    partners += [me.device(y=me.ys(d)) for d in range(1, Y)]
    partners += [me.device(z=me.zs(d)) for d in range(1, Z)]
    for device in partners:
        pl.semaphore_signal(barrier, inc=1, device_id=device, device_id_type=pl.DeviceIdType.MESH)
    pl.semaphore_wait(barrier, len(partners))


class Sender:
    def __init__(self, send, recv):
        self.send, self.recv, self.used, self.copies = send, recv, 0, []

    def start(self, src, dst, device):
        index = self.used
        self.used += 1
        copy = pltpu.make_async_remote_copy(
            src_ref=src, dst_ref=dst, send_sem=self.send.at[index], recv_sem=self.recv.at[index],
            device_id=device, device_id_type=pl.DeviceIdType.MESH)
        copy.start()
        self.copies.append(copy)
        return copy

    def drain(self):
        for copy in self.copies:
            copy.wait_send()


def gather_kernel(block_ref, out, send, recv):
    me = Place()
    x, y, c = me.x, me.y, me.core
    depth_line = pl.ds(ZH * x, ZH)
    yz_line = pl.ds(ZL * y, ZL)
    for half in range(2):
        out[half, me.depth, me.yz, c] = block_ref[:, half * 128:(half + 1) * 128]
    greet(me)
    net = Sender(send, recv)
    sibling = me.device(core=1 - c)

    def share(spot):
        return net.start(out.at[spot], out.at[spot], sibling)

    own = (slice(None), me.depth, me.yz, c)
    phase = [net.start(out.at[own], out.at[own], me.device(z=me.zs(d))) for d in (4, 3, 5, 2, 6, 1, 7)]
    for copy in phase:
        copy.wait_recv()

    spot_a = (0, depth_line, yz_line, c)
    spot_b = (1, depth_line, yz_line, c)
    phase_a = [net.start(out.at[spot_a], out.at[spot_a], me.device(x=me.xs(d))) for d in (2, 1, 3)]
    phase_b = [net.start(out.at[spot_b], out.at[spot_b], me.device(y=me.ys(d))) for d in (2, 1, 3)]
    for copy in phase_a:
        copy.wait_recv()
    unit_a = lambda yy, part=slice(None): (0, part, pl.ds(ZL * yy, ZL), c)
    unit_b = lambda xx, part=slice(None): (1, pl.ds(ZH * xx, ZH), part, c)
    a_up = net.start(out.at[unit_a(y)], out.at[unit_a(y)], me.device(y=me.ys(1)))
    a_down = net.start(out.at[unit_a(y)], out.at[unit_a(y)], me.device(y=me.ys(3)))
    for copy in phase_b:
        copy.wait_recv()
    b_up = net.start(out.at[unit_b(x)], out.at[unit_b(x)], me.device(x=me.xs(1)))
    b_down = net.start(out.at[unit_b(x)], out.at[unit_b(x)], me.device(x=me.xs(3)))
    shared = [share(unit_a(y)), share(unit_b(x))]
    low_d, high_d = pl.ds(0, 4), pl.ds(4, 4)
    low_y, high_y = pl.ds(0, 8), pl.ds(8, 8)
    a_up.wait_recv()
    spot = unit_a(me.ys(3), low_d)
    a_up2 = net.start(out.at[spot], out.at[spot], me.device(y=me.ys(1)))
    a_down.wait_recv()
    spot = unit_a(me.ys(1), high_d)
    a_down2 = net.start(out.at[spot], out.at[spot], me.device(y=me.ys(3)))
    b_up.wait_recv()
    spot = unit_b(me.xs(3), low_y)
    b_up2 = net.start(out.at[spot], out.at[spot], me.device(x=me.xs(1)))
    b_down.wait_recv()
    spot = unit_b(me.xs(1), high_y)
    b_down2 = net.start(out.at[spot], out.at[spot], me.device(x=me.xs(3)))
    shared += [share(unit_a(me.ys(3))), share(unit_a(me.ys(1))), share(unit_b(me.xs(3))), share(unit_b(me.xs(1)))]
    a_up2.wait_recv()
    shared.append(share(unit_a(me.ys(2), low_d)))
    a_down2.wait_recv()
    shared.append(share(unit_a(me.ys(2), high_d)))
    b_up2.wait_recv()
    shared.append(share(unit_b(me.xs(2), low_y)))
    b_down2.wait_recv()
    shared.append(share(unit_b(me.xs(2), high_y)))
    for copy in shared:
        copy.wait_recv()
    net.drain()


def gather(block):
    vmem = pl.BlockSpec(memory_space=pltpu.VMEM)
    copies = 7 + 6 + 4 + 4 + 10
    return pl.pallas_call(
        gather_kernel,
        out_shape=jax.ShapeDtypeStruct((2, X * ZH, Y * ZL, 2, 16, 128), BF16),
        in_specs=[vmem],
        out_specs=vmem,
        scratch_shapes=[pltpu.SemaphoreType.DMA((copies,)), pltpu.SemaphoreType.DMA((copies,))],
        compiler_params=pltpu.CompilerParams(collective_id=0, has_side_effects=True, vmem_limit_bytes=32 * 2**20),
    )(block)


def scatter_kernel(grad, out, acc, inbox, hop_a, hop_b, ring_a, ring_b, line_a, line_b, col, send, recv):
    me = Place()
    x, y, c = me.x, me.y, me.core
    other = 1 - c
    greet(me)
    net = Sender(send, recv)
    sibling = me.device(core=other)

    def unit_a(yy):
        return (0, slice(None), pl.ds(ZL * yy, ZL))

    def unit_b(xx):
        return (1, pl.ds(ZH * xx, ZH), slice(None))

    order = []
    for d in (2, 1, 3, 0):
        order += [unit_a(me.ys(d)), unit_b(me.xs(d))]
    first = [net.start(grad.at[u + (other,)], inbox.at[u], sibling) for u in order]

    def fold(i):
        first[i].wait_recv()
        u = order[i]
        acc[u] = grad[u + (c,)] + inbox[u]

    lo_a = lambda yy: (0, pl.ds(0, 4), pl.ds(ZL * yy, ZL))
    hi_a = lambda yy: (0, pl.ds(4, 4), pl.ds(ZL * yy, ZL))
    lo_b = lambda xx: (1, pl.ds(ZH * xx, ZH), pl.ds(0, 8))
    hi_b = lambda xx: (1, pl.ds(ZH * xx, ZH), pl.ds(8, 8))
    up_y, down_y = me.device(y=me.ys(1)), me.device(y=me.ys(3))
    up_x, down_x = me.device(x=me.xs(1)), me.device(x=me.xs(3))
    fold(0)
    a1 = net.start(acc.at[lo_a(me.ys(2))], hop_a.at[0], up_y)
    a2 = net.start(acc.at[hi_a(me.ys(2))], hop_a.at[1], down_y)
    fold(1)
    b1 = net.start(acc.at[lo_b(me.xs(2))], hop_b.at[0], up_x)
    b2 = net.start(acc.at[hi_b(me.xs(2))], hop_b.at[1], down_x)
    fold(2)
    fold(3)
    a1.wait_recv()
    u = lo_a(me.ys(1))
    acc[u] = acc[u] + hop_a[0]
    a3 = net.start(acc.at[unit_a(me.ys(1))], ring_a.at[0], up_y)
    b1.wait_recv()
    u = lo_b(me.xs(1))
    acc[u] = acc[u] + hop_b[0]
    b3 = net.start(acc.at[unit_b(me.xs(1))], ring_b.at[0], up_x)
    fold(4)
    fold(5)
    a2.wait_recv()
    u = hi_a(me.ys(3))
    acc[u] = acc[u] + hop_a[1]
    a4 = net.start(acc.at[unit_a(me.ys(3))], ring_a.at[1], down_y)
    b2.wait_recv()
    u = hi_b(me.xs(3))
    acc[u] = acc[u] + hop_b[1]
    b4 = net.start(acc.at[unit_b(me.xs(3))], ring_b.at[1], down_x)
    fold(6)
    fold(7)
    a3.wait_recv()
    a4.wait_recv()
    u = unit_a(y)
    acc[u] = acc[u] + ring_a[0] + ring_a[1]
    go_a = []
    for slot, d in enumerate((2, 1, 3)):
        u = (0, pl.ds(ZH * me.xs(d), ZH), pl.ds(ZL * y, ZL))
        go_a.append(net.start(acc.at[u], line_a.at[slot], me.device(x=me.xs(d))))
    b3.wait_recv()
    b4.wait_recv()
    u = unit_b(x)
    acc[u] = acc[u] + ring_b[0] + ring_b[1]
    go_b = []
    for slot, d in enumerate((2, 1, 3)):
        u = (1, pl.ds(ZH * x, ZH), pl.ds(ZL * me.ys(d), ZL))
        go_b.append(net.start(acc.at[u], line_b.at[slot], me.device(y=me.ys(d))))
    for copy in go_a:
        copy.wait_recv()
    u = (0, pl.ds(ZH * x, ZH), pl.ds(ZL * y, ZL))
    acc[u] = acc[u] + (line_a[0] + line_a[1]) + line_a[2]
    for copy in go_b:
        copy.wait_recv()
    u = (1, pl.ds(ZH * x, ZH), pl.ds(ZL * y, ZL))
    acc[u] = acc[u] + (line_b[0] + line_b[1]) + line_b[2]
    last = []
    for slot, d in enumerate((4, 3, 5, 2, 6, 1, 7)):
        z = me.zs(d)
        u = (slice(None), ZH * x + z // ZL, ZL * y + z % ZL)
        last.append(net.start(acc.at[u], col.at[slot], me.device(z=z)))
    total = acc[:, me.depth, me.yz]
    for slot, copy in enumerate(last):
        copy.wait_recv()
        total = total + col[slot]
    for half in range(2):
        out[:, half * 128:(half + 1) * 128] = total[half]
    net.drain()


def scatter(grad):
    vmem = pl.BlockSpec(memory_space=pltpu.VMEM)
    copies = 8 + 8 + 6 + 7
    return pl.pallas_call(
        scatter_kernel,
        out_shape=jax.ShapeDtypeStruct((16, 256), F32),
        in_specs=[vmem],
        out_specs=vmem,
        scratch_shapes=[
            pltpu.VMEM((2, 8, 16, 16, 128), F32),
            pltpu.VMEM((2, 8, 16, 16, 128), F32),
            pltpu.VMEM((2, 4, 4, 16, 128), F32),
            pltpu.VMEM((2, 2, 8, 16, 128), F32),
            pltpu.VMEM((2, 8, 4, 16, 128), F32),
            pltpu.VMEM((2, 2, 16, 16, 128), F32),
            pltpu.VMEM((3, 2, 4, 16, 128), F32),
            pltpu.VMEM((3, 2, 4, 16, 128), F32),
            pltpu.VMEM((7, 2, 16, 128), F32),
            pltpu.SemaphoreType.DMA((copies,)), pltpu.SemaphoreType.DMA((copies,))],
        compiler_params=pltpu.CompilerParams(collective_id=1, has_side_effects=True, vmem_limit_bytes=32 * 2**20),
    )(grad)


def dft_tables(length):
    index = np.arange(length)
    angle = -2.0 * np.pi / length * ((index[:, None] * index[None, :]) % length)
    real, imag = np.cos(angle) / math.sqrt(length), np.sin(angle) / math.sqrt(length)
    full = np.block([[real, imag], [-imag, real]])
    pairs = []
    for matrix in (full, full.T):
        high = matrix.astype(ml_dtypes.bfloat16)
        low = (matrix - high.astype(np.float64)).astype(ml_dtypes.bfloat16)
        pairs.append(np.stack([high, low]))
    return np.stack(pairs)


def split(value):
    high = value.astype(BF16)
    return high, (value - high.astype(F32)).astype(BF16)


def dot(left, right):
    return jnp.dot(left, right, preferred_element_type=F32)


def compute_kernel(factor, group, offsets_ref, order_ref, whole_ref, probe_ref, cos_ref, sin_ref,
                   measured_ref, table_ref, grad_ref, slab, windows, waves, back):
    halves, layers, rows2, lanes = whole_ref.shape
    length = probe_ref.shape[1]
    count = measured_ref.shape[0]
    groups = [tuple(range(first, first + group)) for first in range(0, count, group)]
    lane = lax.broadcasted_iota(jnp.int32, (length, lanes), 1)

    def right_map(blocks, which):
        high_table, low_table = table_ref[which, 0], table_ref[which, 1]
        stacked = jnp.concatenate([jnp.concatenate(pair, axis=1) for pair in blocks], axis=0)
        high, low = split(stacked)
        out = dot(high, high_table) + (dot(low, high_table) + dot(high, low_table))
        return [
            (out[i * length:(i + 1) * length, :length], out[i * length:(i + 1) * length, length:])
            for i in range(len(blocks))
        ]

    def left_map(blocks, which):
        high_table, low_table = table_ref[which, 0], table_ref[which, 1]
        stacked = jnp.concatenate([jnp.concatenate(pair, axis=0) for pair in blocks], axis=1)
        high, low = split(stacked)
        out = dot(high_table, high) + (dot(high_table, low) + dot(low_table, high))
        return [
            (out[:length, i * length:(i + 1) * length], out[length:, i * length:(i + 1) * length])
            for i in range(len(blocks))
        ]

    def forward(blocks):
        return left_map(right_map(blocks, 0), 1)

    def inverse(blocks):
        return left_map(right_map(blocks, 1), 0)

    def times(a, b):
        return (a[0] * b[0] - a[1] * b[1], a[0] * b[1] + a[1] * b[0])

    def conj_times(a, b):
        return (a[0] * b[0] + a[1] * b[1], a[0] * b[1] - a[1] * b[0])

    def load_slab(layer):
        index = order_ref[layer]
        for half in range(halves):
            slab[half] = whole_ref[half, index].astype(F32)

    def load_window(layer, position):
        row, column = offsets_ref[position, 0], offsets_ref[position, 1]
        shift = lax.rem(lanes - column, lanes)
        keep = lane < lanes - column
        parts = []
        for part in range(2):
            first = slab[0, pl.ds(2 * row + part, length, stride=2), :]
            second = slab[1, pl.ds(2 * row + part, length, stride=2), :]
            window = jnp.where(keep, pltpu.roll(first, shift, 1), pltpu.roll(second, shift, 1))
            windows[layer, position, part] = window
            parts.append(window)
        return tuple(parts)

    def add_grad(layer, position, pair):
        index = order_ref[layer]
        row, column = offsets_ref[position, 0], offsets_ref[position, 1]
        shift = lax.rem(column, lanes)
        first = lane >= column
        for part in range(2):
            moved = pltpu.roll(pair[part], shift, 1)
            spot = pl.ds(2 * row + part, length, stride=2)
            grad_ref[0, index, spot, :] += jnp.where(first, moved, 0.0)
            grad_ref[1, index, spot, :] += jnp.where(first, 0.0, moved)

    grad_ref[...] = jnp.zeros_like(grad_ref)
    for position in range(count):
        waves[0, position] = probe_ref[...]

    def wave_of(layer, position):
        return waves[layer, position, 0], waves[layer, position, 1]

    @pl.loop(0, layers - 1)
    def _(layer):
        load_slab(layer)
        medium = (cos_ref[...], sin_ref[...])
        for members in groups:
            blocks = [times(load_window(layer, p), wave_of(layer, p)) for p in members]
            blocks = [times(b, medium) for b in forward(blocks)]
            for p, pair in zip(members, inverse(blocks)):
                waves[layer + 1, p, 0] = pair[0]
                waves[layer + 1, p, 1] = pair[1]

    last = layers - 1
    load_slab(last)
    for members in groups:
        trans = [load_window(last, p) for p in members]
        blocks = [times(t, wave_of(last, p)) for t, p in zip(trans, members)]
        far = forward(blocks)
        scaled = []
        for pair, p in zip(far, members):
            miss = (2.0 * factor) * (pair[0] * pair[0] + pair[1] * pair[1] - measured_ref[p])
            scaled.append((miss * pair[0], miss * pair[1]))
        for p, t, pair in zip(members, trans, inverse(scaled)):
            add_grad(last, p, conj_times(wave_of(last, p), pair))
            pair = conj_times(t, pair)
            back[p, 0] = pair[0]
            back[p, 1] = pair[1]

    @pl.loop(0, layers - 1)
    def _(step):
        layer = layers - 2 - step
        medium = (cos_ref[...], sin_ref[...])
        for members in groups:
            blocks = [(back[p, 0], back[p, 1]) for p in members]
            blocks = [conj_times(medium, b) for b in forward(blocks)]
            for p, pair in zip(members, inverse(blocks)):
                add_grad(layer, p, conj_times(wave_of(layer, p), pair))
                pair = conj_times((windows[layer, p, 0], windows[layer, p, 1]), pair)
                back[p, 0] = pair[0]
                back[p, 1] = pair[1]


def compute(whole, probe, cosine, sine, measured, offsets, order, factor, group=2):
    halves, layers, rows2, lanes = whole.shape
    length = probe.shape[1]
    count = measured.shape[0]
    table = jnp.asarray(dft_tables(length))
    vmem = pl.BlockSpec(memory_space=pltpu.VMEM)
    smem = pl.BlockSpec(memory_space=pltpu.SMEM)
    return pl.pallas_call(
        functools.partial(compute_kernel, factor, group),
        out_shape=jax.ShapeDtypeStruct((halves, layers, rows2, lanes), F32),
        in_specs=[smem, smem] + [vmem] * 6,
        out_specs=vmem,
        scratch_shapes=[
            pltpu.VMEM((halves, rows2, lanes), F32),
            pltpu.VMEM((layers, count, 2, length, length), F32),
            pltpu.VMEM((layers, count, 2, length, length), F32),
            pltpu.VMEM((count, 2, length, length), F32),
        ],
        compiler_params=pltpu.CompilerParams(vmem_limit_bytes=48 * 2**20),
    )(offsets, order, whole, probe, cosine, sine, measured, table)


def per_device(object_slices, probe_wave, propagator_phase, measured, offsets, slice_order):
    width = object_slices.shape[3]
    length = probe_wave.shape[1]
    positions_total = offsets.shape[0] * lax.axis_size("depth") * lax.axis_size("pos")
    factor = 0.25 * width / (length * math.sqrt(positions_total))
    whole = gather(object_slices.reshape(16, width))
    grad = compute(
        whole.reshape(2, 8, 2 * width, 128), probe_wave, jnp.cos(propagator_phase), jnp.sin(propagator_phase),
        measured, offsets, slice_order, factor)
    total = scatter(grad.reshape(2, X * ZH, Y * ZL, 2, 16, 128))
    return total.reshape(object_slices.shape)


def solution(mesh):
    in_specs = (
        P("depth", "pos", None, None),
        P(),
        P(),
        P(("depth", "pos"), None, None),
        P(("depth", "pos"), None),
        P(),
    )
    out_specs = P("depth", "pos", None, None)
    return jax.shard_map(
        per_device, mesh=mesh, in_specs=in_specs, out_specs=out_specs, check_vma=False
    )
```

time: 729 us -> 103 us (0.14); the launches traced: 715 us -> 103 us
  waiting for transfers between devices: 330 us -> 0 us
  matrix products: 183 us -> 0 us
  local copies, waits for them, and re-layouts: 110 us -> 8.9 us
  Pallas kernels: 0 us -> 94.1 us
  blocking collectives: 45.9 us -> 0 us
  other arithmetic: 16.2 us -> 0 us
  between operations: 15.3 us -> 0.03 us
  loops' own time: 15.2 us -> 0 us
    dot_general x240 -> x0, matrix products: 183 us -> none  [the longest x30 29.3 us: fourier_map(): jnp.einsum('jk,pkl->pjl', table_imag, wave_imag, precision=HIGHEST)]
    unnamed x4 -> x0, waiting for transfers between devices: 140 us -> none
    reduce_scatter x1 -> x0, waiting for transfers between devices: 122 us -> none  [per_device(): lax.psum_scatter(partial_grad, 'depth', scatter_dimension=0, tiled=True)]
    pallas_call x0 -> x3, Pallas kernels: none -> 94.1 us  [the longest x1 38.3 us: compute(): pl.pallas_call(functools.partial(compute_kernel, factor, group), out_shap...]
    all_gather x1 -> x0, waiting for transfers between devices: 67.6 us -> none  [per_device(): whole = lax.all_gather(row_blocks, 'depth', axis=0, tiled=True)]
    dynamic_update_slice x8 -> x0, local copies, waits for them, and re-layouts: 55.8 us -> none  [add_window(): return lax.dynamic_update_slice(total, piece, start)]
    all_gather x1 -> x0, blocking collectives: 45.9 us -> none  [per_device(): row_blocks = lax.all_gather(object_slices, 'pos', axis=1, tiled=True)]
    gather x22 -> x0, local copies, waits for them, and re-layouts: 28.3 us -> none
  transfers between devices with their start and end apart: 3 -> 0, of which waited for: 3 -> 0; matrix products, arithmetic and copies ran while one was open for 1% -> 0% of each run, Pallas kernels for 0% -> 0%
where the time goes in v1:
time: 103 us
  Pallas kernels  94.1 us (91%)
  local copies, waits for them, and re-layouts  8.9 us (9%)
    pallas_call x1, Pallas kernels, compute(): pl.pallas_call(functools.partial(compute_kernel, factor, group), out_shap...  38.3 us
    pallas_call x1, Pallas kernels, scatter(): pl.pallas_call(scatter_kernel, out_shape=jax.ShapeDtypeStruct((16, 256),...  28.4 us
    pallas_call x1, Pallas kernels, gather(): pl.pallas_call(gather_kernel, out_shape=jax.ShapeDtypeStruct((2, X * ZH,...  27.4 us
    unnamed x11, local copies, waits for them, and re-layouts  6.5 us

profile of v1, /device:TPU:2, one launch (start us, length us, event | category | flops | bytes accessed | tf_op | source)
XLA Modules:
  0.0 103.0 jit_solution(9453942004036741391)
XLA Ops:
  0.0 0.8 copy.8.offsets_ref
  0.8 0.7 reshape.12.block_ref
  1.5 1.1 %fusion = (f32[128,128]{1,0:T(8,128)S(1)}, f32[128,128]{1,0:T(8,128)S(1)}) fusion(f32[128,128]{1,0:T(8,128)} %param.9), kind=kLoop, calls=%fused_computation | loop fusion | bytes 196608 | tf_op jit(solution)/shard_map/sin | solution.py:438
  2.6 27.4 %shard_map.73 = bf16[2,8,16,2,16,128]{5,4,3,2,1,0:T(8,128)(2,1)S(1)} custom-call(bf16[16,256]{1,0:T(8,128)(2,1)S(1)} %reshape.12.block_ref), custom_call_target="tpu_custom_call" | custom-call | tf_op jit(solution)/shard_map/pallas_call | solution.py:141
  29.9 0.0 copy-start.1
  30.0 1.0 %copy-done.1 = bf16[2,2,256,256]{3,2,1,0:T(8,128)(2,1)S(1)} copy-done((bf16[2,2,256,256]{3,2,1,0:T(8,128)(2,1)S(1)}, bf16[2,2,256,256]{3,2,1,0:T(8,128)(2,1)}, u32[]{:S(2)}) %copy-start.1) | copy-done | bytes 524312
  31.0 0.0 copy-start.2
  31.0 0.9 copy-done.2
  31.9 0.0 copy-start.3
  31.9 0.9 copy-done.3
  32.8 0.0 copy-start.4
  32.8 0.7 copy-done.4
  33.5 38.3 %shard_map.74 = f32[2,8,512,128]{3,2,1,0:T(8,128)} custom-call(s32[4,2]{1,0:T(4,128)S(1)} %copy.8.offsets_ref, s32[8]{0:T(128)S(1)} %copy-done.4, bf16[2,8,512,128]{3,2,1,0:T(8,128)(2,1)S(1)} %bitcast.3, f32[2,128,128]{2,1,0:T(8,128)S(1)} %copy-done.3, f32[128,128]{1,0:T(8,128)S(1)} %get-tuple-element.6.cos_ref, f32[128,128]{1,0:T(8,128)S(1)} %get-tuple-element.5.sin_ref, ...), custom_call_target="tpu_custom_call" | custom-call | tf_op jit(solution)/shard_map/pallas_call | solution.py:416
  71.8 0.0 copy-start
  71.8 2.2 %copy-done = f32[2,8,512,128]{3,2,1,0:T(8,128)S(1)} copy-done((f32[2,8,512,128]{3,2,1,0:T(8,128)S(1)}, f32[2,8,512,128]{3,2,1,0:T(8,128)}, u32[]{:S(2)}) %copy-start) | copy-done | bytes 4194328
  73.9 28.4 %shard_map.75 = f32[16,256]{1,0:T(8,128)S(1)} custom-call(f32[2,8,16,2,16,128]{5,4,3,2,1,0:T(8,128)S(1)} %bitcast.2), custom_call_target="tpu_custom_call" | custom-call | tf_op jit(solution)/shard_map/pallas_call | solution.py:250
  102.4 0.6 reshape.15
Async XLA Ops:
  29.9 1.0 %copy-start.1 = (bf16[2,2,256,256]{3,2,1,0:T(8,128)(2,1)S(1)}, bf16[2,2,256,256]{3,2,1,0:T(8,128)(2,1)}, u32[]{:S(2)}) copy-start(bf16[2,2,256,256]{3,2,1,0:T(8,128)(2,1)} %constant.2.clone.table_ref) | copy-start | bytes 1572868
  31.0 0.9 copy-start.2
  31.9 0.9 copy-start.3
  32.8 0.7 copy-start.4
  71.8 2.2 %copy-start = (f32[2,8,512,128]{3,2,1,0:T(8,128)S(1)}, f32[2,8,512,128]{3,2,1,0:T(8,128)}, u32[]{:S(2)}) copy-start(f32[2,8,512,128]{3,2,1,0:T(8,128)} %shard_map.74) | copy-start | bytes 12582916

commit v2 on v1

--- a/solution.py
+++ b/solution.py
@@ -299,13 +299,12 @@
 
     def right_map(blocks, which):
         high_table, low_table = table_ref[which, 0], table_ref[which, 1]
-        stacked = jnp.concatenate([jnp.concatenate(pair, axis=1) for pair in blocks], axis=0)
-        high, low = split(stacked)
-        out = dot(high, high_table) + (dot(low, high_table) + dot(high, low_table))
-        return [
-            (out[i * length:(i + 1) * length, :length], out[i * length:(i + 1) * length, length:])
-            for i in range(len(blocks))
-        ]
+        results = []
+        for pair in blocks:
+            high, low = split(jnp.concatenate(pair, axis=1))
+            out = dot(high, high_table) + (dot(low, high_table) + dot(high, low_table))
+            results.append((out[:, :length], out[:, length:]))
+        return results
 
     def left_map(blocks, which):
         high_table, low_table = table_ref[which, 0], table_ref[which, 1]
@@ -365,7 +364,7 @@
     def wave_of(layer, position):
         return waves[layer, position, 0], waves[layer, position, 1]
 
-    @pl.loop(0, layers - 1)
+    @pl.loop(0, layers - 1, unroll=7)
     def _(layer):
         load_slab(layer)
         medium = (cos_ref[...], sin_ref[...])
@@ -392,7 +391,7 @@
             back[p, 0] = pair[0]
             back[p, 1] = pair[1]
 
-    @pl.loop(0, layers - 1)
+    @pl.loop(0, layers - 1, unroll=7)
     def _(step):
         layer = layers - 2 - step
         medium = (cos_ref[...], sin_ref[...])
@@ -406,7 +405,7 @@
                 back[p, 1] = pair[1]
 
 
-def compute(whole, probe, cosine, sine, measured, offsets, order, factor, group=2):
+def compute(whole, probe, cosine, sine, measured, offsets, order, factor, group=4):
     halves, layers, rows2, lanes = whole.shape
     length = probe.shape[1]
     count = measured.shape[0]

time: 103 us -> 88.3 us (0.86)
  Pallas kernels: 94.1 us -> 79.1 us
    pallas_call x1, Pallas kernels: 38.3 us -> 23 us  [compute(): pl.pallas_call(functools.partial(compute_kernel, factor, group), out_shap...]
where the time goes in v2:
time: 88.3 us; the launch traced here: 88 us
  Pallas kernels  79.1 us (90%)
  local copies, waits for them, and re-layouts  8.9 us (10%)
    pallas_call x1, Pallas kernels, scatter(): pl.pallas_call(scatter_kernel, out_shape=jax.ShapeDtypeStruct((16, 256),...  28.7 us
    pallas_call x1, Pallas kernels, gather(): pl.pallas_call(gather_kernel, out_shape=jax.ShapeDtypeStruct((2, X * ZH,...  27.4 us
    pallas_call x1, Pallas kernels, compute(): pl.pallas_call(functools.partial(compute_kernel, factor, group), out_shap...  23 us
    unnamed x11, local copies, waits for them, and re-layouts  6.5 us

profile of v2, /device:TPU:2, one launch (start us, length us, event | category | flops | bytes accessed | tf_op | source)
XLA Modules:
  0.0 88.0 jit_solution(12713818644150218501)
XLA Ops:
  0.0 0.8 copy.8.offsets_ref
  0.8 0.7 reshape.12.block_ref
  1.5 1.1 %fusion = (f32[128,128]{1,0:T(8,128)S(1)}, f32[128,128]{1,0:T(8,128)S(1)}) fusion(f32[128,128]{1,0:T(8,128)} %param.9), kind=kLoop, calls=%fused_computation | loop fusion | bytes 196608 | tf_op jit(solution)/shard_map/sin | solution.py:437
  2.6 27.4 %shard_map.73 = bf16[2,8,16,2,16,128]{5,4,3,2,1,0:T(8,128)(2,1)S(1)} custom-call(bf16[16,256]{1,0:T(8,128)(2,1)S(1)} %reshape.12.block_ref), custom_call_target="tpu_custom_call" | custom-call | tf_op jit(solution)/shard_map/pallas_call | solution.py:141
  29.9 0.0 copy-start.1
  30.0 1.0 %copy-done.1 = bf16[2,2,256,256]{3,2,1,0:T(8,128)(2,1)S(1)} copy-done((bf16[2,2,256,256]{3,2,1,0:T(8,128)(2,1)S(1)}, bf16[2,2,256,256]{3,2,1,0:T(8,128)(2,1)}, u32[]{:S(2)}) %copy-start.1) | copy-done | bytes 524312
  31.0 0.0 copy-start.2
  31.0 0.9 %copy-done.2 = f32[4,128,128]{2,1,0:T(8,128)S(1)} copy-done((f32[4,128,128]{2,1,0:T(8,128)S(1)}, f32[4,128,128]{2,1,0:T(8,128)}, u32[]{:S(2)}) %copy-start.2) | copy-done | bytes 262168
  31.9 0.0 copy-start.3
  31.9 0.9 %copy-done.3 = f32[2,128,128]{2,1,0:T(8,128)S(1)} copy-done((f32[2,128,128]{2,1,0:T(8,128)S(1)}, f32[2,128,128]{2,1,0:T(8,128)}, u32[]{:S(2)}) %copy-start.3) | copy-done | bytes 131096
  32.8 0.0 copy-start.4
  32.8 0.7 copy-done.4
  33.5 23.0 %shard_map.74 = f32[2,8,512,128]{3,2,1,0:T(8,128)} custom-call(s32[4,2]{1,0:T(4,128)S(1)} %copy.8.offsets_ref, s32[8]{0:T(128)S(1)} %copy-done.4, bf16[2,8,512,128]{3,2,1,0:T(8,128)(2,1)S(1)} %bitcast.3, f32[2,128,128]{2,1,0:T(8,128)S(1)} %copy-done.3, f32[128,128]{1,0:T(8,128)S(1)} %get-tuple-element.6.cos_ref, f32[128,128]{1,0:T(8,128)S(1)} %get-tuple-element.5.sin_ref, ...), custom_call_target="tpu_custom_call" | custom-call | tf_op jit(solution)/shard_map/pallas_call | solution.py:415
  56.5 0.0 copy-start
  56.5 2.2 %copy-done = f32[2,8,512,128]{3,2,1,0:T(8,128)S(1)} copy-done((f32[2,8,512,128]{3,2,1,0:T(8,128)S(1)}, f32[2,8,512,128]{3,2,1,0:T(8,128)}, u32[]{:S(2)}) %copy-start) | copy-done | bytes 4194328
  58.7 28.7 %shard_map.75 = f32[16,256]{1,0:T(8,128)S(1)} custom-call(f32[2,8,16,2,16,128]{5,4,3,2,1,0:T(8,128)S(1)} %bitcast.2), custom_call_target="tpu_custom_call" | custom-call | tf_op jit(solution)/shard_map/pallas_call | solution.py:250
  87.4 0.6 reshape.15
Async XLA Ops:
  29.9 1.0 %copy-start.1 = (bf16[2,2,256,256]{3,2,1,0:T(8,128)(2,1)S(1)}, bf16[2,2,256,256]{3,2,1,0:T(8,128)(2,1)}, u32[]{:S(2)}) copy-start(bf16[2,2,256,256]{3,2,1,0:T(8,128)(2,1)} %constant.2.clone.table_ref) | copy-start | bytes 1572868
  31.0 0.9 %copy-start.2 = (f32[4,128,128]{2,1,0:T(8,128)S(1)}, f32[4,128,128]{2,1,0:T(8,128)}, u32[]{:S(2)}) copy-start(f32[4,128,128]{2,1,0:T(8,128)} %measured_ref.1) | copy-start | bytes 786436
  31.9 0.9 %copy-start.3 = (f32[2,128,128]{2,1,0:T(8,128)S(1)}, f32[2,128,128]{2,1,0:T(8,128)}, u32[]{:S(2)}) copy-start(f32[2,128,128]{2,1,0:T(8,128)} %probe_ref.1) | copy-start | bytes 393220
  32.8 0.7 copy-start.4
  56.5 2.2 %copy-start = (f32[2,8,512,128]{3,2,1,0:T(8,128)S(1)}, f32[2,8,512,128]{3,2,1,0:T(8,128)}, u32[]{:S(2)}) copy-start(f32[2,8,512,128]{3,2,1,0:T(8,128)} %shard_map.74) | copy-start | bytes 12582916

commit v3 on v0

v3 whole, which is shorter than its diff:
```python
import functools
import math

import jax
import jax.numpy as jnp
import ml_dtypes
import numpy as np
from jax import lax
from jax.experimental import pallas as pl
from jax.experimental.pallas import tpu as pltpu
from jax.sharding import PartitionSpec as P

BF16 = jnp.bfloat16
F32 = jnp.float32
X, ZH, Y, ZL = 4, 2, 4, 4
Z = ZH * ZL
MESH = pl.DeviceIdType.MESH


def dft_tables(length):
    index = np.arange(length)
    angle = -2.0 * np.pi / length * ((index[:, None] * index[None, :]) % length)
    real, imag = np.cos(angle) / math.sqrt(length), np.sin(angle) / math.sqrt(length)
    full = np.block([[real, imag], [-imag, real]])
    pairs = []
    for matrix in (full, full.T):
        high = matrix.astype(ml_dtypes.bfloat16)
        low = (matrix - high.astype(np.float64)).astype(ml_dtypes.bfloat16)
        pairs.append(np.stack([high, low]))
    return np.stack(pairs)


class Place:
    def __init__(self):
        depth, pos = lax.axis_index("depth"), lax.axis_index("pos")
        self.depth = depth
        self.x, self.zh = depth // ZH, depth % ZH
        self.core = pos % 2
        self.yz = pos // 2
        self.y, self.zl = self.yz // ZL, self.yz % ZL
        self.z = self.zh * ZL + self.zl

    def device(self, x=None, y=None, z=None, core=None):
        x = self.x if x is None else x
        y = self.y if y is None else y
        z = self.z if z is None else z
        core = self.core if core is None else core
        return (x * ZH + z // ZL, (y * ZL + z % ZL) * 2 + core)

    def xs(self, d):
        return (self.x + d) % X

    def ys(self, d):
        return (self.y + d) % Y

    def zs(self, d):
        return (self.z + d) % Z


def greet(me):
    barrier = pltpu.get_barrier_semaphore()
    partners = [me.device(core=1 - me.core)]
    partners += [me.device(x=me.xs(d)) for d in range(1, X)]
    partners += [me.device(y=me.ys(d)) for d in range(1, Y)]
    partners += [me.device(z=me.zs(d)) for d in range(1, Z)]
    for device in partners:
        pl.semaphore_signal(barrier, inc=1, device_id=device, device_id_type=MESH)
    pl.semaphore_wait(barrier, len(partners))


class Sender:
    def __init__(self, send, recv):
        self.send, self.recv, self.used, self.copies = send, recv, 0, []

    def start(self, src, dst, device):
        index = self.used
        self.used += 1
        copy = pltpu.make_async_remote_copy(
            src_ref=src, dst_ref=dst, send_sem=self.send.at[index], recv_sem=self.recv.at[index],
            device_id=device, device_id_type=MESH)
        copy.start()
        self.copies.append(copy)
        return copy

    def drain(self):
        for copy in self.copies:
            copy.wait_send()


GATHER_COPIES = 7 + 2 * (3 + 8 + 4) + 2 * 7


def gather_whole(me, net, out, meanwhile):
    x, y, c = me.x, me.y, me.core
    sibling = me.device(core=1 - c)

    def push(spot, device):
        return net.start(out.at[spot], out.at[spot], device)

    own = (slice(None), me.depth, me.yz, c)
    phase = [push(own, me.device(z=me.zs(d))) for d in (4, 3, 5, 2, 6, 1, 7)]
    meanwhile()
    for copy in phase:
        copy.wait_recv()

    def line(half, first, second):
        if half == 0:
            return (0, pl.ds(ZH * first, ZH), pl.ds(ZL * second, ZL), c)
        return (1, pl.ds(ZH * second, ZH), pl.ds(ZL * first, ZL), c)

    def unit(half, second):
        if half == 0:
            return (0, slice(None), pl.ds(ZL * second, ZL), c)
        return (1, pl.ds(ZH * second, ZH), slice(None), c)

    first = (me.xs, me.ys)
    second = (me.ys, me.xs)
    to_first = (lambda d: me.device(x=me.xs(d)), lambda d: me.device(y=me.ys(d)))
    to_second = (lambda d: me.device(y=me.ys(d)), lambda d: me.device(x=me.xs(d)))
    ups, downs, direct = [{}, {}], [{}, {}], [{}, {}]

    def spread(half, d):
        spot = line(half, first[half](d), second[half](0))
        ups[half][d] = push(spot, to_second[half](1))
        downs[half][d] = push(spot, to_second[half](3))

    for half in range(2):
        for d in (1, 3, 2):
            direct[half][d] = push(line(half, first[half](0), second[half](0)), to_first[half](d))
    for half in range(2):
        spread(half, 0)
    for d in (1, 3, 2):
        for half in range(2):
            direct[half][d].wait_recv()
            spread(half, 4 - d)
    shared = [push(unit(half, second[half](0)), sibling) for half in range(2)]
    relayed = []
    for d in (0, 3, 1, 2):
        for half in range(2):
            ups[half][d].wait_recv()
            if d in (0, 2):
                spot = line(half, first[half](d), second[half](3))
                relayed.append((half, d, push(spot, to_second[half](1))))
            downs[half][d].wait_recv()
            if d in (1, 3):
                spot = line(half, first[half](d), second[half](1))
                relayed.append((half, d, push(spot, to_second[half](3))))
    for half in range(2):
        shared.append(push(unit(half, second[half](3)), sibling))
        shared.append(push(unit(half, second[half](1)), sibling))
    for half, d, copy in relayed:
        copy.wait_recv()
        shared.append(push(line(half, first[half](d), second[half](2)), sibling))
    for copy in shared:
        copy.wait_recv()


def split(value):
    high = value.astype(BF16)
    return high, (value - high.astype(F32)).astype(BF16)


def dot(left, right):
    return jnp.dot(left, right, preferred_element_type=F32)


def times(a, b):
    return (a[0] * b[0] - a[1] * b[1], a[0] * b[1] + a[1] * b[0])


def conj_times(a, b):
    return (a[0] * b[0] + a[1] * b[1], a[0] * b[1] - a[1] * b[0])


def kernel(factor, offsets_ref, order_ref, block_ref, probe_hbm, phase_hbm, measured_hbm, table_hbm, out_ref,
           whole, probe_ref, phase_ref, measured_ref, table_ref, medium, slab, windows, waves, pend, place_ref,
           grads, inbox, acc, hop, ring, line, piece, stage, xbox, pair, zbox, final,
           load_sem, send, recv, s1_send, s1_recv, hop_send, hop_recv, ring_send, ring_recv, line_send, line_recv,
           end_send, end_recv):
    layers = order_ref.shape[0]
    count, length = measured_ref.shape[:2]
    lanes = whole.shape[-1]
    field = 2 * lanes
    me = Place()
    x, y, c = me.x, me.y, me.core
    other = 1 - c
    net = Sender(send, recv)
    loads = [
        pltpu.make_async_copy(src, dst, load_sem.at[i])
        for i, (src, dst) in enumerate((
            (phase_hbm, phase_ref), (probe_hbm, probe_ref), (table_hbm, table_ref), (measured_hbm, measured_ref)))
    ]
    for load in loads:
        load.start()
    for half in range(2):
        whole[half, me.depth, me.yz, c] = block_ref[:, half * lanes:(half + 1) * lanes]
    greet(me)
    lane = lax.broadcasted_iota(jnp.int32, (length, lanes), 1)

    def prepare():
        for load in loads:
            load.wait()
        medium[0] = jnp.cos(phase_ref[...])
        medium[1] = jnp.sin(phase_ref[...])
        rows = lax.broadcasted_iota(jnp.int32, (field, length), 0)
        inner = lax.broadcasted_iota(jnp.int32, (field, length), 1)
        for p in range(count):
            hit = rows - inner == offsets_ref[p, 0]
            place_ref[:, p * length:(p + 1) * length] = jnp.where(hit, 1.0, 0.0).astype(BF16)
            waves[0, p] = probe_ref[...]

    gather_whole(me, net, whole, prepare)

    def right_map(blocks, which):
        high_table, low_table = table_ref[which, 0], table_ref[which, 1]
        results = []
        for block in blocks:
            high, low = split(jnp.concatenate(block, axis=1))
            out = dot(high, high_table) + (dot(low, high_table) + dot(high, low_table))
            results.append((out[:, :length], out[:, length:]))
        return results

    def left_map(blocks, which):
        high_table, low_table = table_ref[which, 0], table_ref[which, 1]
        stacked = jnp.concatenate([jnp.concatenate(block, axis=0) for block in blocks], axis=1)
        high, low = split(stacked)
        out = dot(high_table, high) + (dot(high_table, low) + dot(low_table, high))
        return [
            (out[:length, i * length:(i + 1) * length], out[length:, i * length:(i + 1) * length])
            for i in range(len(blocks))
        ]

    def forward(blocks):
        return left_map(right_map(blocks, 0), 1)

    def inverse(blocks):
        return left_map(right_map(blocks, 1), 0)

    def load_windows(layer):
        index = order_ref[layer]
        for half in range(2):
            slab[half] = whole[half, index].reshape(2 * field, lanes).astype(F32)
        for p in range(count):
            row, column = offsets_ref[p, 0], offsets_ref[p, 1]
            shift = lax.rem(lanes - column, lanes)
            keep = lane < lanes - column
            for part in range(2):
                left = slab[0, pl.ds(2 * row + part, length, stride=2), :]
                right = slab[1, pl.ds(2 * row + part, length, stride=2), :]
                windows[layer, p, part] = jnp.where(keep, pltpu.roll(left, shift, 1), pltpu.roll(right, shift, 1))

    def window_of(layer, p):
        return windows[layer, p, 0], windows[layer, p, 1]

    def wave_of(layer, p):
        return waves[layer, p, 0], waves[layer, p, 1]

    def add_grads(j, slot):
        layer = layers - 1 - j
        terms = [conj_times(wave_of(layer, p), (pend[slot, p, 0], pend[slot, p, 1])) for p in range(count)]
        for part in range(2):
            moved = []
            for p in range(count):
                column = offsets_ref[p, 1]
                turned = pltpu.roll(terms[p][part], lax.rem(column, lanes), 1)
                moved.append(jnp.concatenate(
                    [jnp.where(lane >= column, turned, 0.0), jnp.where(lane >= column, 0.0, turned)], axis=1))
            high, low = split(jnp.concatenate(moved, axis=0))
            total = dot(place_ref[...], high) + dot(place_ref[...], low)
            for half in range(2):
                grads[j, half, part] = total[:, half * lanes:(half + 1) * lanes].reshape(Y * ZL, 2, 8, lanes)

    def remote(src, dst, send_sem, recv_sem, device):
        return pltpu.make_async_remote_copy(
            src_ref=src, dst_ref=dst, send_sem=send_sem, recv_sem=recv_sem, device_id=device, device_id_type=MESH)

    def y_unit(d):
        return pl.ds(ZL * me.ys(d), ZL)

    def share(j):
        return remote(grads.at[j, :, :, :, other], inbox.at[j], s1_send.at[j], s1_recv.at[j], me.device(core=other))

    def hop_of(j, side):
        return remote(acc.at[j, side, :, y_unit(2)], hop.at[j, side], hop_send.at[j, side], hop_recv.at[j, side],
                      me.device(y=me.ys(1 + 2 * side)))

    def ring_of(j, side):
        return remote(acc.at[j, :, :, y_unit(1 + 2 * side)], ring.at[j, side], ring_send.at[j, side],
                      ring_recv.at[j, side], me.device(y=me.ys(1 + 2 * side)))

    def lines(j):
        result = []
        for d in range(1, ZL):
            zl = (me.zl + d) % ZL
            result.append(remote(acc.at[j, :, :, ZL * y + zl], line.at[j, d - 1], line_send.at[j, d - 1],
                                 line_recv.at[j, d - 1], me.device(z=me.zh * ZL + zl)))
        return result

    def do_share(j):
        share(j).start()

    def do_fold(j):
        share(j).wait_recv()
        acc[j] = grads[j, :, :, :, c] + inbox[j]
        for side in range(2):
            hop_of(j, side).start()

    def do_ring(j):
        for side, d in ((0, 1), (1, 3)):
            hop_of(j, side).wait_recv()
            acc[j, side, :, y_unit(d)] = acc[j, side, :, y_unit(d)] + hop[j, side]
            ring_of(j, side).start()

    def do_line(j):
        for side in range(2):
            ring_of(j, side).wait_recv()
        acc[j, :, :, y_unit(0)] = acc[j, :, :, y_unit(0)] + ring[j, 0] + ring[j, 1]
        for copy in lines(j):
            copy.start()

    def do_piece(j):
        for copy in lines(j):
            copy.wait_recv()
        piece[j] = acc[j, :, :, me.yz] + line[j, 0] + line[j, 1] + line[j, 2]

    load_windows(0)

    @pl.loop(0, layers - 1)
    def _(layer):
        load_windows(layer + 1)
        field_factor = (medium[0], medium[1])
        blocks = [times(window_of(layer, p), wave_of(layer, p)) for p in range(count)]
        blocks = [times(b, field_factor) for b in forward(blocks)]
        for p, block in enumerate(inverse(blocks)):
            waves[layer + 1, p, 0] = block[0]
            waves[layer + 1, p, 1] = block[1]

    last = layers - 1
    blocks = [times(window_of(last, p), wave_of(last, p)) for p in range(count)]
    scaled = []
    for p, block in enumerate(forward(blocks)):
        miss = (2.0 * factor) * (block[0] * block[0] + block[1] * block[1] - measured_ref[p])
        scaled.append((miss * block[0], miss * block[1]))
    for p, block in enumerate(inverse(scaled)):
        pend[0, p, 0] = block[0]
        pend[0, p, 1] = block[1]

    @pl.loop(0, layers - 1)
    def _(i):
        @pl.when(i >= 6)
        def _():
            do_line(i - 6)

        @pl.when(i >= 4)
        def _():
            do_ring(i - 4)

        @pl.when(i >= 2)
        def _():
            do_fold(i - 2)

        @pl.when(i >= 1)
        def _():
            do_share(i - 1)

        slot = lax.rem(i, 2)
        layer = layers - 2 - i
        field_factor = (medium[0], medium[1])
        blocks = [conj_times(window_of(layer + 1, p), (pend[slot, p, 0], pend[slot, p, 1])) for p in range(count)]
        blocks = [conj_times(field_factor, b) for b in forward(blocks)]
        blocks = inverse(blocks)
        add_grads(i, slot)
        for p, block in enumerate(blocks):
            pend[1 - slot, p, 0] = block[0]
            pend[1 - slot, p, 1] = block[1]

    do_share(6)
    add_grads(7, 1)
    do_share(7)
    do_fold(5)
    do_ring(3)
    do_line(1)
    do_fold(6)
    do_ring(4)
    do_line(2)
    do_fold(7)
    do_ring(5)
    do_line(3)
    do_piece(0)
    do_ring(6)
    do_line(4)
    do_piece(1)
    do_ring(7)
    do_line(5)
    do_piece(2)
    do_line(6)
    do_piece(3)
    do_line(7)
    for j in range(4, 8):
        do_piece(j)

    for s in range(layers):
        inverse_index = jnp.zeros((), jnp.int32)
        for k in range(layers):
            inverse_index = jnp.where(order_ref[k] == s, layers - 1 - k, inverse_index)
        stage[s] = piece[inverse_index]
    to_x = [remote(stage.at[pl.ds(ZH * me.xs(d), ZH)], xbox.at[d - 1], end_send.at[d - 1], end_recv.at[d - 1],
                   me.device(x=me.xs(d))) for d in range(1, X)]
    for copy in to_x:
        copy.start()
    for copy in to_x:
        copy.wait_recv()
    pair[...] = stage[pl.ds(ZH * x, ZH)] + xbox[0] + xbox[1] + xbox[2]
    to_z = remote(pair.at[1 - me.zh], zbox, end_send.at[3], end_recv.at[3], me.device(z=me.zs(4)))
    to_z.start()
    to_z.wait_recv()
    total = pair[me.zh] + zbox[...]
    for half in range(2):
        for part in range(2):
            final[half, pl.ds(part, 8, stride=2), :] = total[half, part]
        out_ref[:, half * lanes:(half + 1) * lanes] = final[half]

    net.drain()
    for j in range(layers):
        for copy in [share(j)] + [f(j, side) for f in (hop_of, ring_of) for side in range(2)] + lines(j):
            copy.wait_send()
    for copy in to_x + [to_z]:
        copy.wait_send()


def per_device(object_slices, probe_wave, propagator_phase, measured, offsets, slice_order):
    layers = slice_order.shape[0]
    width = object_slices.shape[3]
    length = probe_wave.shape[1]
    count = offsets.shape[0]
    positions_total = count * lax.axis_size("depth") * lax.axis_size("pos")
    factor = 0.25 * width / (length * math.sqrt(positions_total))
    table = jnp.asarray(dft_tables(length))
    vmem = pl.BlockSpec(memory_space=pltpu.VMEM)
    smem = pl.BlockSpec(memory_space=pltpu.SMEM)
    anywhere = pl.BlockSpec(memory_space=pl.ANY)
    dma = pltpu.SemaphoreType.DMA
    block = (2, 2, 8, 128)
    total = pl.pallas_call(
        functools.partial(kernel, factor),
        out_shape=jax.ShapeDtypeStruct((16, width), F32),
        in_specs=[smem, smem, vmem] + [anywhere] * 4,
        out_specs=vmem,
        scratch_shapes=[
            pltpu.VMEM((2, layers, Y * ZL, 2, 16, 128), BF16),
            pltpu.VMEM((2, length, length), F32),
            pltpu.VMEM((length, length), F32),
            pltpu.VMEM((count, length, length), F32),
            pltpu.VMEM((2, 2, 2 * length, 2 * length), BF16),
            pltpu.VMEM((2, length, length), F32),
            pltpu.VMEM((2, 2 * width, 128), F32),
            pltpu.VMEM((layers, count, 2, length, length), F32),
            pltpu.VMEM((layers, count, 2, length, length), F32),
            pltpu.VMEM((2, count, 2, length, length), F32),
            pltpu.VMEM((width, count * length), BF16),
            pltpu.VMEM((layers, 2, 2, Y * ZL, 2, 8, 128), F32),
            pltpu.VMEM((layers, 2, 2, Y * ZL, 8, 128), F32),
            pltpu.VMEM((layers, 2, 2, Y * ZL, 8, 128), F32),
            pltpu.VMEM((layers, 2, 2, ZL, 8, 128), F32),
            pltpu.VMEM((layers, 2, 2, 2, ZL, 8, 128), F32),
            pltpu.VMEM((layers, 3) + block, F32),
            pltpu.VMEM((layers,) + block, F32),
            pltpu.VMEM((layers,) + block, F32),
            pltpu.VMEM((3, 2) + block, F32),
            pltpu.VMEM((2,) + block, F32),
            pltpu.VMEM(block, F32),
            pltpu.VMEM((2, 16, 128), F32),
            dma((4,)), dma((GATHER_COPIES,)), dma((GATHER_COPIES,)),
            dma((layers,)), dma((layers,)),
            dma((layers, 2)), dma((layers, 2)), dma((layers, 2)), dma((layers, 2)),
            dma((layers, 3)), dma((layers, 3)), dma((4,)), dma((4,)),
        ],
        compiler_params=pltpu.CompilerParams(collective_id=0, has_side_effects=True, vmem_limit_bytes=56 * 2**20),
    )(offsets, slice_order, object_slices.reshape(16, width), probe_wave, propagator_phase, measured, table)
    return total.reshape(object_slices.shape)


def solution(mesh):
    in_specs = (
        P("depth", "pos", None, None),
        P(),
        P(),
        P(("depth", "pos"), None, None),
        P(("depth", "pos"), None),
        P(),
    )
    out_specs = P("depth", "pos", None, None)
    return jax.shard_map(
        per_device, mesh=mesh, in_specs=in_specs, out_specs=out_specs, check_vma=False
    )
```

time: 729 us -> 82.5 us (0.11); the launches traced: 715 us -> 82 us
  waiting for transfers between devices: 330 us -> 0 us
  matrix products: 183 us -> 0 us
  local copies, waits for them, and re-layouts: 110 us -> 3.98 us
  Pallas kernels: 0 us -> 78 us
  blocking collectives: 45.9 us -> 0 us
  other arithmetic: 16.2 us -> 0 us
  between operations: 15.3 us -> 0.01 us
  loops' own time: 15.2 us -> 0 us
    dot_general x240 -> x0, matrix products: 183 us -> none  [the longest x30 29.3 us: fourier_map(): jnp.einsum('jk,pkl->pjl', table_imag, wave_imag, precision=HIGHEST)]
    unnamed x4 -> x0, waiting for transfers between devices: 140 us -> none
    reduce_scatter x1 -> x0, waiting for transfers between devices: 122 us -> none  [per_device(): lax.psum_scatter(partial_grad, 'depth', scatter_dimension=0, tiled=True)]
    pallas_call x0 -> x1, Pallas kernels: none -> 78 us  [per_device(): pl.pallas_call(functools.partial(kernel, factor), out_shape=jax.ShapeDtyp...]
    all_gather x1 -> x0, waiting for transfers between devices: 67.6 us -> none  [per_device(): whole = lax.all_gather(row_blocks, 'depth', axis=0, tiled=True)]
    dynamic_update_slice x8 -> x0, local copies, waits for them, and re-layouts: 55.8 us -> none  [add_window(): return lax.dynamic_update_slice(total, piece, start)]
    all_gather x1 -> x0, blocking collectives: 45.9 us -> none  [per_device(): row_blocks = lax.all_gather(object_slices, 'pos', axis=1, tiled=True)]
    gather x22 -> x0, local copies, waits for them, and re-layouts: 28.3 us -> none
  transfers between devices with their start and end apart: 3 -> 0, of which waited for: 3 -> 0; matrix products, arithmetic and copies ran while one was open for 1% -> 0% of each run, Pallas kernels for 0% -> 0%
where the time goes in v3:
time: 82.5 us; the launch traced here: 82 us
  Pallas kernels  78 us (95%)
  local copies, waits for them, and re-layouts  3.98 us (5%)
    pallas_call x1, Pallas kernels, per_device(): pl.pallas_call(functools.partial(kernel, factor), out_shape=jax.ShapeDtyp...  78 us

profile of v3, /device:TPU:2, one launch (start us, length us, event | category | flops | bytes accessed | tf_op | source)
XLA Modules:
  0.0 82.0 jit_solution(14491780108403254137)
XLA Ops:
  0.0 1.3 %copy.8.offsets_ref = s32[4,2]{1,0:T(4,128)} copy(s32[4,2]{0,1:T(2,128)} %param.11) | data formatting | bytes 64 | tf_op args[4]
  1.3 1.3 %reshape.6.block_ref = bf16[16,256]{1,0:T(8,128)(2,1)} reshape(bf16[1,8,2,256]{3,2,1,0:T(2,128)(2,1)} %param.7) | data formatting | bytes 16384 | tf_op jit(solution)/shard_map/reshape | solution.py:479
  2.6 78.0 %shard_map.73 = f32[16,256]{1,0:T(8,128)} custom-call(s32[4,2]{1,0:T(4,128)} %copy.8.offsets_ref, s32[8]{0:T(128)} %order_ref.1, bf16[16,256]{1,0:T(8,128)(2,1)} %reshape.6.block_ref, f32[2,128,128]{2,1,0:T(8,128)} %probe_hbm.1, f32[128,128]{1,0:T(8,128)} %phase_hbm.1, f32[4,128,128]{2,1,0:T(8,128)} %measured_hbm.1, ...), custom_call_target="tpu_custom_call" | custom-call | tf_op jit(solution)/shard_map/pallas_call | solution.py:444
  80.6 1.3 %reshape.7 = f32[1,8,2,256]{3,2,1,0:T(2,128)} reshape(f32[16,256]{1,0:T(8,128)} %shard_map.73) | data formatting | bytes 32768 | tf_op jit(solution)/shard_map/reshape | solution.py:480

commit v4 on v3

--- a/solution.py
+++ b/solution.py
@@ -15,6 +15,7 @@
 X, ZH, Y, ZL = 4, 2, 4, 4
 Z = ZH * ZL
 MESH = pl.DeviceIdType.MESH
+RING, LINE = 5, 7
 
 
 def dft_tables(length):
@@ -68,91 +69,68 @@
     pl.semaphore_wait(barrier, len(partners))
 
 
-class Sender:
-    def __init__(self, send, recv):
-        self.send, self.recv, self.used, self.copies = send, recv, 0, []
-
-    def start(self, src, dst, device):
-        index = self.used
-        self.used += 1
-        copy = pltpu.make_async_remote_copy(
-            src_ref=src, dst_ref=dst, send_sem=self.send.at[index], recv_sem=self.recv.at[index],
-            device_id=device, device_id_type=MESH)
-        copy.start()
-        self.copies.append(copy)
-        return copy
-
-    def drain(self):
-        for copy in self.copies:
-            copy.wait_send()
-
-
-GATHER_COPIES = 7 + 2 * (3 + 8 + 4) + 2 * 7
-
-
-def gather_whole(me, net, out, meanwhile):
+def settle(ref, sem):
+    pltpu.make_async_copy(ref, ref, sem).wait()
+
+
+def remote(src, dst, send_sem, recv_sem, device):
+    return pltpu.make_async_remote_copy(
+        src_ref=src, dst_ref=dst, send_sem=send_sem, recv_sem=recv_sem, device_id=device, device_id_type=MESH)
+
+
+def gather_whole(me, out, send, recv, meanwhile):
     x, y, c = me.x, me.y, me.core
-    sibling = me.device(core=1 - c)
-
-    def push(spot, device):
-        return net.start(out.at[spot], out.at[spot], device)
+
+    def push(spot, send_sem, recv_sem, device):
+        remote(out.at[spot], out.at[spot], send.at[send_sem], recv.at[recv_sem], device).start()
 
     own = (slice(None), me.depth, me.yz, c)
-    phase = [push(own, me.device(z=me.zs(d))) for d in (4, 3, 5, 2, 6, 1, 7)]
+    for d in (4, 3, 5, 2, 6, 1, 7):
+        push(own, 0, 0, me.device(z=me.zs(d)))
     meanwhile()
-    for copy in phase:
-        copy.wait_recv()
-
-    def line(half, first, second):
-        if half == 0:
-            return (0, pl.ds(ZH * first, ZH), pl.ds(ZL * second, ZL), c)
-        return (1, pl.ds(ZH * second, ZH), pl.ds(ZL * first, ZL), c)
+    seven = out.at[:, pl.ds(0, 1), pl.ds(0, 7), 0]
+    settle(seven, recv.at[0])
+
+    first = (me.xs, me.ys)
+    second = (me.ys, me.xs)
+    to_first = (lambda d: me.device(x=me.xs(d)), lambda d: me.device(y=me.ys(d)))
+    to_second = (lambda d: me.device(y=me.ys(d)), lambda d: me.device(x=me.xs(d)))
+
+    def line(half):
+        return (half, pl.ds(ZH * x, ZH), pl.ds(ZL * y, ZL), c)
 
     def unit(half, second):
         if half == 0:
             return (0, slice(None), pl.ds(ZL * second, ZL), c)
         return (1, pl.ds(ZH * second, ZH), slice(None), c)
 
-    first = (me.xs, me.ys)
-    second = (me.ys, me.xs)
-    to_first = (lambda d: me.device(x=me.xs(d)), lambda d: me.device(y=me.ys(d)))
-    to_second = (lambda d: me.device(y=me.ys(d)), lambda d: me.device(x=me.xs(d)))
-    ups, downs, direct = [{}, {}], [{}, {}], [{}, {}]
-
-    def spread(half, d):
-        spot = line(half, first[half](d), second[half](0))
-        ups[half][d] = push(spot, to_second[half](1))
-        downs[half][d] = push(spot, to_second[half](3))
-
+    three_lines = out.at[0, pl.ds(0, 3), pl.ds(0, 8), 0]
+    three_units = out.at[0, pl.ds(0, 6), :, 0]
+    for d in (2, 1, 3):
+        for half in range(2):
+            push(line(half), 1 + half, 1 + half, to_first[half](d))
     for half in range(2):
-        for d in (1, 3, 2):
-            direct[half][d] = push(line(half, first[half](0), second[half](0)), to_first[half](d))
+        settle(three_lines, recv.at[1 + half])
+        for d in (2, 1, 3):
+            push(unit(half, second[half](0)), 3 + half, 4 + 3 * half + d, to_second[half](d))
     for half in range(2):
-        spread(half, 0)
+        push(unit(half, second[half](0)), 5 + half, 3 + half * 8, me.device(core=1 - c))
     for d in (1, 3, 2):
         for half in range(2):
-            direct[half][d].wait_recv()
-            spread(half, 4 - d)
-    shared = [push(unit(half, second[half](0)), sibling) for half in range(2)]
-    relayed = []
-    for d in (0, 3, 1, 2):
+            spot = unit(half, second[half](4 - d))
+            settle(out.at[spot], recv.at[4 + 3 * half + d])
+            push(spot, 5 + half, 3 + half * 8, me.device(core=1 - c))
+    for half in range(2):
+        settle(out.at[half, :, :, 1 - c], recv.at[3 + half * 8])
+
+    def drain():
+        settle(seven, send.at[0])
         for half in range(2):
-            ups[half][d].wait_recv()
-            if d in (0, 2):
-                spot = line(half, first[half](d), second[half](3))
-                relayed.append((half, d, push(spot, to_second[half](1))))
-            downs[half][d].wait_recv()
-            if d in (1, 3):
-                spot = line(half, first[half](d), second[half](1))
-                relayed.append((half, d, push(spot, to_second[half](3))))
-    for half in range(2):
-        shared.append(push(unit(half, second[half](3)), sibling))
-        shared.append(push(unit(half, second[half](1)), sibling))
-    for half, d, copy in relayed:
-        copy.wait_recv()
-        shared.append(push(line(half, first[half](d), second[half](2)), sibling))
-    for copy in shared:
-        copy.wait_recv()
+            settle(three_lines, send.at[1 + half])
+            settle(three_units, send.at[3 + half])
+            settle(out.at[half, :, :, c], send.at[5 + half])
+
+    return drain
 
 
 def split(value):
@@ -184,7 +162,6 @@
     me = Place()
     x, y, c = me.x, me.y, me.core
     other = 1 - c
-    net = Sender(send, recv)
     loads = [
         pltpu.make_async_copy(src, dst, load_sem.at[i])
         for i, (src, dst) in enumerate((
@@ -192,8 +169,9 @@
     ]
     for load in loads:
         load.start()
-    for half in range(2):
-        whole[half, me.depth, me.yz, c] = block_ref[:, half * lanes:(half + 1) * lanes]
+    for row in range(block_ref.shape[1]):
+        for half in range(2):
+            whole[half, me.depth, me.yz, c, 2 * row:2 * row + 2] = block_ref[0, row, :, half * lanes:(half + 1) * lanes]
     greet(me)
     lane = lax.broadcasted_iota(jnp.int32, (length, lanes), 1)
 
@@ -205,11 +183,11 @@
         rows = lax.broadcasted_iota(jnp.int32, (field, length), 0)
         inner = lax.broadcasted_iota(jnp.int32, (field, length), 1)
         for p in range(count):
-            hit = rows - inner == offsets_ref[p, 0]
+            hit = rows - inner == offsets_ref[0, p]
             place_ref[:, p * length:(p + 1) * length] = jnp.where(hit, 1.0, 0.0).astype(BF16)
             waves[0, p] = probe_ref[...]
 
-    gather_whole(me, net, whole, prepare)
+    drain_gather = gather_whole(me, whole, send, recv, prepare)
 
     def right_map(blocks, which):
         high_table, low_table = table_ref[which, 0], table_ref[which, 1]
@@ -241,7 +219,7 @@
         for half in range(2):
             slab[half] = whole[half, index].reshape(2 * field, lanes).astype(F32)
         for p in range(count):
-            row, column = offsets_ref[p, 0], offsets_ref[p, 1]
+            row, column = offsets_ref[0, p], offsets_ref[1, p]
             shift = lax.rem(lanes - column, lanes)
             keep = lane < lanes - column
             for part in range(2):
@@ -261,7 +239,7 @@
         for part in range(2):
             moved = []
             for p in range(count):
-                column = offsets_ref[p, 1]
+                column = offsets_ref[1, p]
                 turned = pltpu.roll(terms[p][part], lax.rem(column, lanes), 1)
                 moved.append(jnp.concatenate(
                     [jnp.where(lane >= column, turned, 0.0), jnp.where(lane >= column, 0.0, turned)], axis=1))
@@ -270,57 +248,38 @@
             for half in range(2):
                 grads[j, half, part] = total[:, half * lanes:(half + 1) * lanes].reshape(Y * ZL, 2, 8, lanes)
 
-    def remote(src, dst, send_sem, recv_sem, device):
-        return pltpu.make_async_remote_copy(
-            src_ref=src, dst_ref=dst, send_sem=send_sem, recv_sem=recv_sem, device_id=device, device_id_type=MESH)
-
     def y_unit(d):
         return pl.ds(ZL * me.ys(d), ZL)
 
-    def share(j):
-        return remote(grads.at[j, :, :, :, other], inbox.at[j], s1_send.at[j], s1_recv.at[j], me.device(core=other))
-
-    def hop_of(j, side):
-        return remote(acc.at[j, side, :, y_unit(2)], hop.at[j, side], hop_send.at[j, side], hop_recv.at[j, side],
-                      me.device(y=me.ys(1 + 2 * side)))
-
-    def ring_of(j, side):
-        return remote(acc.at[j, :, :, y_unit(1 + 2 * side)], ring.at[j, side], ring_send.at[j, side],
-                      ring_recv.at[j, side], me.device(y=me.ys(1 + 2 * side)))
-
-    def lines(j):
-        result = []
-        for d in range(1, ZL):
-            zl = (me.zl + d) % ZL
-            result.append(remote(acc.at[j, :, :, ZL * y + zl], line.at[j, d - 1], line_send.at[j, d - 1],
-                                 line_recv.at[j, d - 1], me.device(z=me.zh * ZL + zl)))
-        return result
-
     def do_share(j):
-        share(j).start()
+        remote(grads.at[j, :, :, :, other], inbox.at[j], s1_send.at[0], s1_recv.at[j], me.device(core=other)).start()
 
     def do_fold(j):
-        share(j).wait_recv()
+        settle(inbox.at[j], s1_recv.at[j])
         acc[j] = grads[j, :, :, :, c] + inbox[j]
         for side in range(2):
-            hop_of(j, side).start()
+            remote(acc.at[j, side, :, y_unit(2)], hop.at[j, side], hop_send.at[0], hop_recv.at[j, side],
+                   me.device(y=me.ys(1 + 2 * side))).start()
 
     def do_ring(j):
-        for side, d in ((0, 1), (1, 3)):
-            hop_of(j, side).wait_recv()
-            acc[j, side, :, y_unit(d)] = acc[j, side, :, y_unit(d)] + hop[j, side]
-            ring_of(j, side).start()
+        for side in range(2):
+            unit = y_unit(1 + 2 * side)
+            settle(hop.at[j, side], hop_recv.at[j, side])
+            acc[j, side, :, unit] = acc[j, side, :, unit] + hop[j, side]
+            remote(acc.at[j, :, :, unit], ring.at[j, side], ring_send.at[0], ring_recv.at[j, side],
+                   me.device(y=me.ys(1 + 2 * side))).start()
 
     def do_line(j):
         for side in range(2):
-            ring_of(j, side).wait_recv()
+            settle(ring.at[j, side], ring_recv.at[j, side])
         acc[j, :, :, y_unit(0)] = acc[j, :, :, y_unit(0)] + ring[j, 0] + ring[j, 1]
-        for copy in lines(j):
-            copy.start()
+        for d in (2, 3, 1):
+            zl = (me.zl + d) % ZL
+            remote(acc.at[j, :, :, ZL * y + zl], line.at[j, d - 1], line_send.at[0], line_recv.at[j],
+                   me.device(z=me.zh * ZL + zl)).start()
 
     def do_piece(j):
-        for copy in lines(j):
-            copy.wait_recv()
+        settle(line.at[j], line_recv.at[j])
         piece[j] = acc[j, :, :, me.yz] + line[j, 0] + line[j, 1] + line[j, 2]
 
     load_windows(0)
@@ -347,17 +306,17 @@
 
     @pl.loop(0, layers - 1)
     def _(i):
-        @pl.when(i >= 6)
+        @pl.when(i >= LINE)
         def _():
-            do_line(i - 6)
-
-        @pl.when(i >= 4)
+            do_line(i - LINE)
+
+        @pl.when(i >= RING)
         def _():
-            do_ring(i - 4)
-
-        @pl.when(i >= 2)
+            do_ring(i - RING)
+
+        @pl.when(i >= 3)
         def _():
-            do_fold(i - 2)
+            do_fold(i - 3)
 
         @pl.when(i >= 1)
         def _():
@@ -377,26 +336,27 @@
     do_share(6)
     add_grads(7, 1)
     do_share(7)
+    do_fold(4)
     do_fold(5)
-    do_ring(3)
-    do_line(1)
+    for j in range(7 - RING, 4):
+        do_ring(j)
     do_fold(6)
+    drain_gather()
+    do_fold(7)
     do_ring(4)
-    do_line(2)
-    do_fold(7)
     do_ring(5)
+    for j in range(7 - LINE, 3):
+        do_line(j)
+    do_ring(6)
     do_line(3)
-    do_piece(0)
-    do_ring(6)
     do_line(4)
-    do_piece(1)
     do_ring(7)
     do_line(5)
-    do_piece(2)
     do_line(6)
-    do_piece(3)
+    for j in range(5):
+        do_piece(j)
     do_line(7)
-    for j in range(4, 8):
+    for j in range(5, 8):
         do_piece(j)
 
     for s in range(layers):
@@ -404,28 +364,24 @@
         for k in range(layers):
             inverse_index = jnp.where(order_ref[k] == s, layers - 1 - k, inverse_index)
         stage[s] = piece[inverse_index]
-    to_x = [remote(stage.at[pl.ds(ZH * me.xs(d), ZH)], xbox.at[d - 1], end_send.at[d - 1], end_recv.at[d - 1],
-                   me.device(x=me.xs(d))) for d in range(1, X)]
-    for copy in to_x:
-        copy.start()
-    for copy in to_x:
-        copy.wait_recv()
+    for d in (2, 1, 3):
+        remote(stage.at[pl.ds(ZH * me.xs(d), ZH)], xbox.at[d - 1], end_send.at[0], end_recv.at[0],
+               me.device(x=me.xs(d))).start()
+    settle(inbox, s1_send.at[0])
+    settle(hop, hop_send.at[0])
+    settle(xbox, end_recv.at[0])
     pair[...] = stage[pl.ds(ZH * x, ZH)] + xbox[0] + xbox[1] + xbox[2]
-    to_z = remote(pair.at[1 - me.zh], zbox, end_send.at[3], end_recv.at[3], me.device(z=me.zs(4)))
+    to_z = remote(pair.at[1 - me.zh], zbox, end_send.at[1], end_recv.at[1], me.device(z=me.zs(4)))
     to_z.start()
-    to_z.wait_recv()
+    settle(ring, ring_send.at[0])
+    settle(line, line_send.at[0])
+    settle(xbox, end_send.at[0])
+    to_z.wait()
     total = pair[me.zh] + zbox[...]
     for half in range(2):
         for part in range(2):
             final[half, pl.ds(part, 8, stride=2), :] = total[half, part]
         out_ref[:, half * lanes:(half + 1) * lanes] = final[half]
-
-    net.drain()
-    for j in range(layers):
-        for copy in [share(j)] + [f(j, side) for f in (hop_of, ring_of) for side in range(2)] + lines(j):
-            copy.wait_send()
-    for copy in to_x + [to_z]:
-        copy.wait_send()
 
 
 def per_device(object_slices, probe_wave, propagator_phase, measured, offsets, slice_order):
@@ -470,13 +426,12 @@
             pltpu.VMEM((2,) + block, F32),
             pltpu.VMEM(block, F32),
             pltpu.VMEM((2, 16, 128), F32),
-            dma((4,)), dma((GATHER_COPIES,)), dma((GATHER_COPIES,)),
-            dma((layers,)), dma((layers,)),
-            dma((layers, 2)), dma((layers, 2)), dma((layers, 2)), dma((layers, 2)),
-            dma((layers, 3)), dma((layers, 3)), dma((4,)), dma((4,)),
+            dma((4,)), dma((7,)), dma((12,)),
+            dma((1,)), dma((layers,)), dma((1,)), dma((layers, 2)), dma((1,)), dma((layers, 2)),
+            dma((1,)), dma((layers,)), dma((2,)), dma((2,)),
         ],
         compiler_params=pltpu.CompilerParams(collective_id=0, has_side_effects=True, vmem_limit_bytes=56 * 2**20),
-    )(offsets, slice_order, object_slices.reshape(16, width), probe_wave, propagator_phase, measured, table)
+    )(offsets.T, slice_order, object_slices, probe_wave, propagator_phase, measured, table)
     return total.reshape(object_slices.shape)
 
 

time: 82.5 us -> 77.2 us (0.936)
  local copies, waits for them, and re-layouts: 3.98 us -> 1.34 us
  Pallas kernels: 78 us -> 75.6 us
    pallas_call x1, Pallas kernels: 78 us -> 75.6 us  [per_device(): pl.pallas_call(functools.partial(kernel, factor), out_shape=jax.ShapeDtyp...]
    unnamed x1 -> x0, local copies, waits for them, and re-layouts: 1.34 us -> none
    reshape x1 -> x0, local copies, waits for them, and re-layouts: 1.3 us -> none  [per_device(): object_slices.reshape(16, width)]
where the time goes in v4:
time: 77.2 us; the launch traced here: 77 us
  Pallas kernels  75.6 us (98%)
  local copies, waits for them, and re-layouts  1.34 us (2%)
    pallas_call x1, Pallas kernels, per_device(): pl.pallas_call(functools.partial(kernel, factor), out_shape=jax.ShapeDtyp...  75.6 us

profile of v4, /device:TPU:2, one launch (start us, length us, event | category | flops | bytes accessed | tf_op | source)
XLA Modules:
  0.0 77.0 jit_solution(16133267108176712530)
XLA Ops:
  0.0 75.6 %shard_map.73 = f32[16,256]{1,0:T(8,128)} custom-call(s32[2,4]{1,0:T(2,128)} %bitcast.1, s32[8]{0:T(128)} %order_ref.1, bf16[1,8,2,256]{3,2,1,0:T(2,128)(2,1)} %block_ref.1, f32[2,128,128]{2,1,0:T(8,128)} %probe_hbm.1, f32[128,128]{1,0:T(8,128)} %phase_hbm.1, f32[4,128,128]{2,1,0:T(8,128)} %measured_hbm.1, bf16[2,2,256,256]{3,2,1,0:T(8,128)(2,1)} %constant.2.clone.table_hbm), custom_call_target="tpu_custom_call" | custom-call | tf_op jit(solution)/shard_map/pallas_call | solution.py:400
  75.6 1.3 %reshape.3 = f32[1,8,2,256]{3,2,1,0:T(2,128)} reshape(f32[16,256]{1,0:T(8,128)} %shard_map.73) | data formatting | bytes 32768 | tf_op jit(solution)/shard_map/reshape | solution.py:435

commit v5 on v4

--- a/solution.py
+++ b/solution.py
@@ -284,7 +284,7 @@
 
     load_windows(0)
 
-    @pl.loop(0, layers - 1)
+    @pl.loop(0, layers - 1, unroll=7)
     def _(layer):
         load_windows(layer + 1)
         field_factor = (medium[0], medium[1])

time: 77.2 us -> 76.4 us (0.990)
  Pallas kernels: 75.6 us -> 74.8 us
    pallas_call x1, Pallas kernels: 75.6 us -> 74.8 us  [per_device(): pl.pallas_call(functools.partial(kernel, factor), out_shape=jax.ShapeDtyp...]
where the time goes in v5:
time: 76.4 us; the launch traced here: 76.2 us
  Pallas kernels  74.8 us (98%)
  local copies, waits for them, and re-layouts  1.34 us (2%)
    pallas_call x1, Pallas kernels, per_device(): pl.pallas_call(functools.partial(kernel, factor), out_shape=jax.ShapeDtyp...  74.8 us

profile of v5, /device:TPU:2, one launch (start us, length us, event | category | flops | bytes accessed | tf_op | source)
XLA Modules:
  0.0 76.2 jit_solution(16167247326901459373)
XLA Ops:
  0.0 74.8 %shard_map.73 = f32[16,256]{1,0:T(8,128)} custom-call(s32[2,4]{1,0:T(2,128)} %bitcast.1, s32[8]{0:T(128)} %order_ref.1, bf16[1,8,2,256]{3,2,1,0:T(2,128)(2,1)} %block_ref.1, f32[2,128,128]{2,1,0:T(8,128)} %probe_hbm.1, f32[128,128]{1,0:T(8,128)} %phase_hbm.1, f32[4,128,128]{2,1,0:T(8,128)} %measured_hbm.1, bf16[2,2,256,256]{3,2,1,0:T(8,128)(2,1)} %constant.2.clone.table_hbm), custom_call_target="tpu_custom_call" | custom-call | tf_op jit(solution)/shard_map/pallas_call | solution.py:400
  74.8 1.3 %reshape.3 = f32[1,8,2,256]{3,2,1,0:T(2,128)} reshape(f32[16,256]{1,0:T(8,128)} %shard_map.73) | data formatting | bytes 32768 | tf_op jit(solution)/shard_map/reshape | solution.py:435

commit v6 on v5

--- a/solution.py
+++ b/solution.py
@@ -15,6 +15,7 @@
 X, ZH, Y, ZL = 4, 2, 4, 4
 Z = ZH * ZL
 MESH = pl.DeviceIdType.MESH
+DEPTH_STEPS = ((2, ZL), (1, ZL), (3, ZL), (0, ZL), (2, 0), (1, 0), (3, 0))
 RING, LINE = 5, 7
 
 
@@ -64,6 +65,7 @@
     partners += [me.device(x=me.xs(d)) for d in range(1, X)]
     partners += [me.device(y=me.ys(d)) for d in range(1, Y)]
     partners += [me.device(z=me.zs(d)) for d in range(1, Z)]
+    partners += [me.device(x=me.xs(d), z=me.zs(ZL)) for d in range(1, X)]
     for device in partners:
         pl.semaphore_signal(barrier, inc=1, device_id=device, device_id_type=MESH)
     pl.semaphore_wait(barrier, len(partners))
@@ -152,7 +154,7 @@
 
 def kernel(factor, offsets_ref, order_ref, block_ref, probe_hbm, phase_hbm, measured_hbm, table_hbm, out_ref,
            whole, probe_ref, phase_ref, measured_ref, table_ref, medium, slab, windows, waves, pend, place_ref,
-           grads, inbox, acc, hop, ring, line, piece, stage, xbox, pair, zbox, final,
+           grads, inbox, acc, hop, ring, line, piece, stage, box, final,
            load_sem, send, recv, s1_send, s1_recv, hop_send, hop_recv, ring_send, ring_recv, line_send, line_recv,
            end_send, end_recv):
     layers = order_ref.shape[0]
@@ -364,24 +366,23 @@
         for k in range(layers):
             inverse_index = jnp.where(order_ref[k] == s, layers - 1 - k, inverse_index)
         stage[s] = piece[inverse_index]
-    for d in (2, 1, 3):
-        remote(stage.at[pl.ds(ZH * me.xs(d), ZH)], xbox.at[d - 1], end_send.at[0], end_recv.at[0],
-               me.device(x=me.xs(d))).start()
+    for i, (dx, dz) in enumerate(DEPTH_STEPS):
+        target = me.xs(dx) * ZH + me.zs(dz) // ZL
+        remote(stage.at[target], box.at[i], end_send.at[0], end_recv.at[0],
+               me.device(x=me.xs(dx), z=me.zs(dz))).start()
     settle(inbox, s1_send.at[0])
     settle(hop, hop_send.at[0])
-    settle(xbox, end_recv.at[0])
-    pair[...] = stage[pl.ds(ZH * x, ZH)] + xbox[0] + xbox[1] + xbox[2]
-    to_z = remote(pair.at[1 - me.zh], zbox, end_send.at[1], end_recv.at[1], me.device(z=me.zs(4)))
-    to_z.start()
     settle(ring, ring_send.at[0])
     settle(line, line_send.at[0])
-    settle(xbox, end_send.at[0])
-    to_z.wait()
-    total = pair[me.zh] + zbox[...]
+    settle(box, end_recv.at[0])
+    total = stage[me.depth]
+    for i in range(len(DEPTH_STEPS)):
+        total = total + box[i]
     for half in range(2):
         for part in range(2):
             final[half, pl.ds(part, 8, stride=2), :] = total[half, part]
         out_ref[:, half * lanes:(half + 1) * lanes] = final[half]
+    settle(box, end_send.at[0])
 
 
 def per_device(object_slices, probe_wave, propagator_phase, measured, offsets, slice_order):
@@ -422,9 +423,7 @@
             pltpu.VMEM((layers, 3) + block, F32),
             pltpu.VMEM((layers,) + block, F32),
             pltpu.VMEM((layers,) + block, F32),
-            pltpu.VMEM((3, 2) + block, F32),
-            pltpu.VMEM((2,) + block, F32),
-            pltpu.VMEM(block, F32),
+            pltpu.VMEM((7,) + block, F32),
             pltpu.VMEM((2, 16, 128), F32),
             dma((4,)), dma((7,)), dma((12,)),
             dma((1,)), dma((layers,)), dma((1,)), dma((layers, 2)), dma((1,)), dma((layers, 2)),

time: 76.4 us -> 77.1 us (level); the launches traced: 76.2 us -> 75.7 us
  no operation moved by 1% of the time
where the time goes in v6:
time: 77.1 us; the launch traced here: 75.7 us
  Pallas kernels  74.4 us (96%)
  local copies, waits for them, and re-layouts  1.34 us (2%)
    pallas_call x1, Pallas kernels, per_device(): pl.pallas_call(functools.partial(kernel, factor), out_shape=jax.ShapeDtyp...  74.4 us

profile of v6, /device:TPU:2, one launch (start us, length us, event | category | flops | bytes accessed | tf_op | source)
XLA Modules:
  0.0 75.7 jit_solution(8223115630780695819)
XLA Ops:
  0.0 74.4 %shard_map.73 = f32[16,256]{1,0:T(8,128)} custom-call(s32[2,4]{1,0:T(2,128)} %bitcast.1, s32[8]{0:T(128)} %order_ref.1, bf16[1,8,2,256]{3,2,1,0:T(2,128)(2,1)} %block_ref.1, f32[2,128,128]{2,1,0:T(8,128)} %probe_hbm.1, f32[128,128]{1,0:T(8,128)} %phase_hbm.1, f32[4,128,128]{2,1,0:T(8,128)} %measured_hbm.1, bf16[2,2,256,256]{3,2,1,0:T(8,128)(2,1)} %constant.2.clone.table_hbm), custom_call_target="tpu_custom_call" | custom-call | tf_op jit(solution)/shard_map/pallas_call | solution.py:401
  74.4 1.3 %reshape.3 = f32[1,8,2,256]{3,2,1,0:T(2,128)} reshape(f32[16,256]{1,0:T(8,128)} %shard_map.73) | data formatting | bytes 32768 | tf_op jit(solution)/shard_map/reshape | solution.py:434
